TPU v7x, 32 devices: a whole 2x2x4 slice. The times are simulated.
32 devices in a mesh: dp: 8 (over y, x, core), expert: 4 (over z).
Axes of the slice: x: 2, y: 2, z: 4, core: 2. Of those that a mesh axis runs over, the one named last changes fastest.
Arguments:
- tokens: bfloat16 [1024, 2048], P('dp', 'expert'), may hold values from -6 to 6
- route_weight: bfloat16 [1024, 8], P('dp'), may hold values from 0.049804688 to 0.44921875
- expert_ids: int32 [1024, 8], P('dp'), may hold values from 0 to 7, all different within a row; in each aligned block of 128 rows (0 to 127, 128 to 255, ...) at most 128 rows name the same one
- gate_weight: bfloat16 [4, 1536, 2048], P('expert', 'dp'), may hold values from -0.125 to 0.125
- up_weight: bfloat16 [4, 1536, 2048], P('expert', 'dp'), may hold values from -0.125 to 0.125
- down_weight: bfloat16 [4, 1536, 2048], P('expert', 'dp'), may hold values from -0.21875 to 0.21875
- grad_output: bfloat16 [1024, 2048], P('dp', 'expert'), may hold values from -1.75 to 1.75
Outputs:
- mixed: bfloat16 [1024, 2048], P('dp', 'expert')
- grad_tokens: bfloat16 [1024, 2048], P('dp', 'expert')
- grad_route: float32 [1024, 8], P(('dp', 'expert'))
- grad_gate: bfloat16 [4, 1536, 2048], P('expert', 'dp')
- grad_up: bfloat16 [4, 1536, 2048], P('expert', 'dp')
- grad_down: bfloat16 [4, 1536, 2048], P('expert', 'dp')
Inputs may be any that keep to these rules, and one draw needn't show every extreme that they name: `expert_ids`: each token names 8 different experts; among the 128 tokens of one device's aligned block no expert is named more than 128 times, a bound that some block reaches.
All inputs are finite; a program needn't handle non-finite values.
Results may differ from a plain program's by a relative error of at most 0.015.
Values may be sent and summed in bfloat16 or wider, within the bound.
A program may use at most 64 MiB of HBM per device.

v0:
```python
import jax
import jax.numpy as jnp
from jax import lax
from jax.sharding import PartitionSpec as P

PIECES = 4


def contract_last(left_side, right_side):
    return lax.dot_general(
        left_side, right_side, (((1,), (1,)), ((), ())), preferred_element_type=jnp.float32
    )


def contract_first(left_side, right_side):
    return lax.dot_general(
        left_side, right_side, (((0,), (0,)), ((), ())), preferred_element_type=jnp.float32
    )


def silu_parts(gate_act):
    sigmoid_val = jax.nn.sigmoid(gate_act)
    return (gate_act * sigmoid_val, sigmoid_val * (1.0 + gate_act * (1.0 - sigmoid_val)))


def expert_forward(slot_rows, slot_scale, gate_piece, up_piece, down_piece):
    gate_act = contract_last(slot_rows, gate_piece)
    up_act = contract_last(slot_rows, up_piece)
    active, silu_slope = silu_parts(gate_act)
    hidden = (active * up_act).astype(jnp.bfloat16)
    partial_out = jnp.dot(hidden, down_piece, preferred_element_type=jnp.float32)
    scaled = (slot_scale.astype(jnp.float32)[:, None] * partial_out).astype(jnp.bfloat16)
    return (scaled, gate_act, up_act, hidden)


def on_device(tokens, route_weight, expert_ids, gate_weight, up_weight, down_weight, grad_output):
    groups = lax.axis_size("expert")
    group_index = lax.axis_index("expert")
    data_size = lax.axis_size("dp")
    exp_local = data_size // PIECES
    tok_local, topk_count = expert_ids.shape
    capacity = min(tok_local, 2 * tok_local * topk_count // (exp_local * groups))
    full_tokens, full_grad = (
        lax.all_gather(tokens, "expert", axis=1, tiled=True),
        lax.all_gather(grad_output, "expert", axis=1, tiled=True),
    )
    feature_width = full_tokens.shape[1]
    gate_piece = gate_weight[0]
    up_piece = up_weight[0]
    down_piece = down_weight[0]
    flat_ids = expert_ids.reshape(-1)
    row_count = flat_ids.shape[0]
    owned_rows = flat_ids // exp_local == group_index
    local_ids = flat_ids % exp_local
    chosen = (
        (local_ids[:, None] == jnp.arange(exp_local, dtype=jnp.int32)[None, :])
        & owned_rows[:, None]
    ).astype(jnp.int32)
    slot_ranks = jnp.sum(chosen * (jnp.cumsum(chosen, axis=0) - 1), axis=1)
    slot_count = exp_local * capacity
    slot_pos = jnp.where(owned_rows, local_ids * capacity + slot_ranks, slot_count)
    row_index = jnp.arange(row_count, dtype=jnp.int32)
    row_of = jnp.zeros((slot_count,), jnp.int32).at[slot_pos].set(row_index, mode="drop")
    slot_live = (
        jnp.zeros((slot_count,), jnp.int32).at[slot_pos].set(jnp.ones_like(row_index), mode="drop")
    )
    token_of = row_of // topk_count
    keep_mask = slot_live.astype(tokens.dtype)[:, None]
    slot_weight = route_weight.reshape(-1)[row_of] * slot_live.astype(route_weight.dtype)

    def spread(values):
        trailing = values.shape[1:]
        grouped = values.reshape((exp_local, 1, capacity) + trailing)
        return jnp.broadcast_to(grouped, (exp_local, PIECES, capacity) + trailing).reshape(
            (data_size, capacity) + trailing
        )

    send_rows = spread(full_tokens[token_of] * keep_mask)
    send_weight = spread(slot_weight)
    send_grads = spread(full_grad[token_of] * keep_mask)
    recv_grads = None
    recv_scale = None
    recv_rows, recv_weight = (
        lax.all_to_all(send_rows, "dp", split_axis=0, concat_axis=0, tiled=True),
        lax.all_to_all(send_weight, "dp", split_axis=0, concat_axis=0, tiled=True),
    )
    scaled, gate_act, up_act, hidden = expert_forward(
        recv_rows.reshape(-1, feature_width),
        recv_weight.reshape(-1),
        gate_piece,
        up_piece,
        down_piece,
    )
    returned = lax.all_to_all(
        scaled.reshape(data_size, capacity, feature_width),
        "dp",
        split_axis=0,
        concat_axis=0,
        tiled=True,
    )
    slot_rows = recv_rows.reshape(-1, feature_width)
    wide_token = spread(token_of).reshape(-1)
    wide_live = spread(slot_live).reshape(-1)
    wide_row = spread(row_of).reshape(-1)
    token_place = (
        (wide_token[None, :] == jnp.arange(tok_local, dtype=jnp.int32)[:, None])
        & (wide_live[None, :] > 0)
    ).astype(jnp.bfloat16)
    mixed_sum = jnp.dot(
        token_place, returned.reshape(-1, feature_width), preferred_element_type=jnp.float32
    )
    recv_grads, recv_scale = (
        lax.all_to_all(send_grads, "dp", split_axis=0, concat_axis=0, tiled=True),
        lax.all_to_all(send_weight, "dp", split_axis=0, concat_axis=0, tiled=True),
    )
    active, silu_slope = silu_parts(gate_act)
    slot_grads = recv_grads.reshape(-1, feature_width)
    weight_wide = recv_scale.reshape(-1).astype(jnp.float32)[:, None]
    into_hidden = contract_last(slot_grads, down_piece)
    route_terms = jnp.sum(into_hidden * hidden.astype(jnp.float32), axis=1).astype(jnp.bfloat16)
    hidden_grad = weight_wide * into_hidden
    gate_grad = (hidden_grad * up_act * silu_slope).astype(jnp.bfloat16)
    up_grad = (hidden_grad * active).astype(jnp.bfloat16)
    row_grad = (
        jnp.dot(gate_grad, gate_piece, preferred_element_type=jnp.float32)
        + jnp.dot(up_grad, up_piece, preferred_element_type=jnp.float32)
    ).astype(jnp.bfloat16)
    scaled_grad = (weight_wide * slot_grads.astype(jnp.float32)).astype(jnp.bfloat16)
    grad_gate = contract_first(gate_grad, slot_rows).astype(jnp.bfloat16)[None]
    grad_up = contract_first(up_grad, slot_rows).astype(jnp.bfloat16)[None]
    grad_down = contract_first(hidden, scaled_grad).astype(jnp.bfloat16)[None]
    back_rows, back_terms = (
        lax.all_to_all(
            row_grad.reshape(data_size, capacity, feature_width),
            "dp",
            split_axis=0,
            concat_axis=0,
            tiled=True,
        ),
        lax.all_to_all(
            route_terms.reshape(data_size, capacity), "dp", split_axis=0, concat_axis=0, tiled=True
        ),
    )
    token_sum = jnp.dot(
        token_place, back_rows.reshape(-1, feature_width), preferred_element_type=jnp.float32
    )
    row_place = (
        (wide_row[None, :] == jnp.arange(row_count, dtype=jnp.int32)[:, None])
        & (wide_live[None, :] > 0)
    ).astype(jnp.bfloat16)
    route_sum = jnp.dot(
        row_place, back_terms.reshape(-1), preferred_element_type=jnp.float32
    ).reshape(tok_local, topk_count)
    mixed_part, token_part, route_part = (
        lax.psum_scatter(mixed_sum, "expert", scatter_dimension=1, tiled=True),
        lax.psum_scatter(token_sum, "expert", scatter_dimension=1, tiled=True),
        lax.psum_scatter(route_sum, "expert", scatter_dimension=0, tiled=True),
    )
    return (
        mixed_part.astype(jnp.bfloat16),
        token_part.astype(jnp.bfloat16),
        route_part,
        grad_gate,
        grad_up,
        grad_down,
    )


def solution(mesh):
    return jax.shard_map(
        on_device,
        mesh=mesh,
        in_specs=(
            P("dp", "expert"),
            P("dp", None),
            P("dp", None),
            P("expert", "dp", None),
            P("expert", "dp", None),
            P("expert", "dp", None),
            P("dp", "expert"),
        ),
        out_specs=(
            P("dp", "expert"),
            P("dp", "expert"),
            P(("dp", "expert"), None),
            P("expert", "dp", None),
            P("expert", "dp", None),
            P("expert", "dp", None),
        ),
        check_vma=False,
    )
```

profile of v0, /device:TPU:0, one launch (start us, length us, event | category | flops | bytes accessed | tf_op | source)
XLA Modules:
  0.0 337.5 jit_solution(11932268879961076054)
XLA Ops:
  7.2 0.0 copy-start
  7.2 0.9 copy.22
  8.0 0.1 reshape.320
  8.1 0.1 reshape.319
  8.2 0.1 reshape.318
  8.4 0.8 copy.25
  9.2 0.1 reshape.322
  9.3 0.6 reduce-window.6
  9.9 0.2 slice_reduce_fusion
  10.1 0.2 reduce-window.9
  10.3 0.1 add_bitcast_fusion
  10.5 4.3 %scatter_custom_fusion.1 = s32[256]{0:T(256)S(1)} fusion(s32[1024]{0:T(1024)S(1)} %bitcast.103, s32[1024]{0:T(1024)S(1)} %rem.84, s32[]{:T(128)} %constant.55.clone.1), kind=kCustom, calls=%fused_computation.95 | custom fusion | bytes 1028 | tf_op jit(solution)/shard_map/scatter | solution.py:65
  14.8 4.3 %scatter_custom_fusion = s32[256]{0:T(256)S(1)} fusion(s32[1024]{0:T(1024)S(1)} %bitcast.104, s32[1024]{0:T(1024)S(1)} %iota.26, s32[]{:T(128)} %constant.55.clone.1), kind=kCustom, calls=%fused_computation.97 | custom fusion | bytes 1028 | tf_op jit(solution)/shard_map/scatter | solution.py:63
  19.1 1.9 gather_fusion
  21.1 0.6 copy.26
  21.7 5.2 %all-to-all-start = ((bf16[8,1,128]{2,1,0:T(2,128)(2,1)}), bf16[8,1,128]{2,1,0:T(2,128)(2,1)S(1)}, u32[]{:S(2)}, u32[]{:S(2)}) async-start(bf16[8,1,128]{2,1,0:T(2,128)(2,1)} %copy.26), calls=%async_computation | async-start | bytes 8192 | tf_op jit(solution)/shard_map/all_to_all | solution.py:85
  26.9 16.8 %all_gather.6 = bf16[128,2048]{1,0:T(8,128)(2,1)S(1)} all-gather(bf16[128,512]{1,0:T(8,128)(2,1)} %param.7), channel_id=1, replica_groups=mesh['dp'=8,'expert'=4] {'expert'}, dimensions={1}, use_global_device_ids=true | all-gather | bytes 655360 | tf_op jit(solution)/shard_map/all_gather | solution.py:44
  43.6 15.7 %all_gather.7 = bf16[128,2048]{1,0:T(8,128)(2,1)S(1)} all-gather(bf16[128,512]{1,0:T(8,128)(2,1)} %param.13), channel_id=1, replica_groups=mesh['dp'=8,'expert'=4] {'expert'}, dimensions={1}, use_global_device_ids=true | all-gather | bytes 655360 | tf_op jit(solution)/shard_map/all_gather | solution.py:45
  59.3 2.3 gather_fusion.1
  61.7 2.4 gather_fusion.2
  64.1 1.7 broadcast_multiply_fusion.1
  65.8 0.0 all-to-all-done
  65.8 0.5 broadcast_in_dim.75
  66.3 53.4 %all_to_all.36 = bf16[8,128,2048]{2,1,0:T(8,128)(2,1)} all-to-all(bf16[8,128,2048]{2,1,0:T(8,128)(2,1)S(1)} %bitcast.90), channel_id=1, replica_groups=mesh['dp'=8,'expert'=4] {'dp'}, dimensions={0} | all-to-all | bytes 8388608 | tf_op jit(solution)/shard_map/all_to_all | solution.py:84
  119.8 2.5 broadcast_in_dim.76
  122.3 4.7 %all-to-all-start.3 = ((bf16[8,128,2048]{2,1,0:T(8,128)(2,1)}), bf16[8,128,2048]{2,1,0:T(8,128)(2,1)}, u32[]{:S(2)}, u32[]{:S(2)}) async-start(bf16[8,128,2048]{2,1,0:T(8,128)(2,1)} %bitcast.89), calls=%async_computation.4 | async-start | bytes 8388608 | tf_op jit(solution)/shard_map/all_to_all | solution.py:113
  127.0 0.0 copy-start.1
  127.0 0.0 copy-start.3
  127.0 0.0 copy-done.4
  127.0 4.8 %fusion.14 = f32[1024,192]{0,1:T(8,128)} fusion(bf16[1024,2048]{1,0:T(8,128)(2,1)} %bitcast.85, bf16[1,192,2048]{2,1,0:T(8,128)(2,1)S(1)} %copy-done.4), kind=kOutput, calls=%fused_computation.25 | convolution fusion | flops 805306368 | bytes 5767168 | tf_op jit(solution)/shard_map/dot_general | solution.py:10
  131.8 0.0 copy-done.1
  131.8 0.0 copy-done.3
  131.8 2.5 fusion.18
  134.2 41.9 %all-to-all-done.3 = bf16[8,128,2048]{2,1,0:T(8,128)(2,1)} async-done(((bf16[8,128,2048]{2,1,0:T(8,128)(2,1)}), bf16[8,128,2048]{2,1,0:T(8,128)(2,1)}, u32[]{:S(2)}, u32[]{:S(2)}) %all-to-all-start.3) | async-done | bytes 4194336 | tf_op jit(solution)/shard_map/all_to_all | solution.py:113
  176.1 0.0 copy-done
  176.1 5.2 %multiply_reduce_fusion = (bf16[1024]{0:T(1024)(128)(2,1)S(1)}, bf16[1024,192]{0,1:T(8,128)(2,1)}, bf16[1024,192]{0,1:T(8,128)(2,1)S(1)}, bf16[1024,192]{0,1:T(8,128)(2,1)S(1)}) fusion(f32[1024,192]{0,1:T(8,128)} %fusion.14, f32[1024,192]{0,1:T(8,128)} %fusion.18, f32[1024]{0:T(1024)S(1)} %bitcast.107, bf16[1024,2048]{1,0:T(8,128)(2,1)} %bitcast.21, ...), kind=kOutput, calls=%fused_computation.31 | convolution fusion | flops 809040896 | bytes 7739392 | tf_op jit(solution)/shard_map/dot_general | solution.py:10
  181.3 0.6 copy.27
  181.9 3.3 all-to-all-start.5
  185.2 4.3 %multiply_convert_fusion.1 = bf16[1024,2048]{1,0:T(8,128)(2,1)} fusion(bf16[1024,192]{0,1:T(8,128)(2,1)} %get-tuple-element.7, f32[1024]{0:T(1024)S(1)} %bitcast.108, bf16[1,192,2048]{2,1,0:T(8,128)(2,1)S(1)} %copy-done), kind=kOutput, calls=%fused_computation.7 | convolution fusion | flops 809500672 | bytes 5378048 | tf_op jit(solution)/shard_map/dot_general | solution.py:31
  189.5 0.2 all-to-all-done.5
  189.7 4.7 %all-to-all-start.2 = ((bf16[8,128,2048]{2,1,0:T(8,128)(2,1)}), bf16[8,128,2048]{2,1,0:T(8,128)(2,1)}, u32[]{:S(2)}, u32[]{:S(2)}) async-start(bf16[8,128,2048]{2,1,0:T(8,128)(2,1)} %bitcast.94), calls=%async_computation.2 | async-start | bytes 8388608 | tf_op jit(solution)/shard_map/all_to_all | solution.py:94
  194.4 1.3 fusion.16
  195.7 3.3 add_convert_fusion
  199.0 44.4 %all-to-all-done.2 = bf16[8,128,2048]{2,1,0:T(8,128)(2,1)} async-done(((bf16[8,128,2048]{2,1,0:T(8,128)(2,1)}), bf16[8,128,2048]{2,1,0:T(8,128)(2,1)}, u32[]{:S(2)}, u32[]{:S(2)}) %all-to-all-start.2) | async-done | bytes 4194336 | tf_op jit(solution)/shard_map/all_to_all | solution.py:94
  243.4 4.6 %all-to-all-start.4 = ((bf16[8,128,2048]{2,1,0:T(8,128)(2,1)}), bf16[8,128,2048]{2,1,0:T(8,128)(2,1)}, u32[]{:S(2)}, u32[]{:S(2)}) async-start(bf16[8,128,2048]{2,1,0:T(8,128)(2,1)} %bitcast.91), calls=%async_computation.5 | async-start | bytes 8388608 | tf_op jit(solution)/shard_map/all_to_all | solution.py:133
  248.0 0.0 reduce-scatter.10.cloned.1.call-start
  248.1 5.4 %fusion.2 = f32[1,128,8]{2,0,1:T(1,128)} fusion(s32[128,8]{1,0:T(8,128)S(1)} %multiply_add_fusion, s32[1024]{0:T(1024)S(1)} %bitcast.105, pred[1024]{0:T(1024)(128)(4,1)S(1)} %bitcast.100, bf16[8,1,128]{2,1,0:T(2,128)(2,1)S(1)} %all-to-all-done.5), kind=kOutput, calls=%fused_computation.11 | convolution fusion | flops 4194304 | bytes 15360 | tf_op jit(solution)/shard_map/dot_general | solution.py:151
  253.5 0.0 reduce-scatter.10.cloned.1.call-update
  253.5 0.0 reduce-scatter.6.cloned.1.call-start
  253.6 3.9 %fusion.24 = f32[128,2048]{1,0:T(8,128)} fusion(bf16[1024,2048]{1,0:T(8,128)(2,1)} %bitcast.18, s32[1024]{0:T(1024)S(1)} %bitcast.96, pred[1024]{0:T(1024)(128)(4,1)S(1)} %bitcast.101), kind=kOutput, calls=%fused_computation.42 | convolution fusion | flops 537133056 | bytes 5248000 | tf_op jit(solution)/shard_map/dot_general | solution.py:109
  257.5 0.0 reduce-scatter.6.cloned.1.call-update
  257.5 0.0 reduce-scatter.8.cloned.1.call-start
  257.5 39.6 %all-to-all-done.4 = bf16[8,128,2048]{2,1,0:T(8,128)(2,1)} async-done(((bf16[8,128,2048]{2,1,0:T(8,128)(2,1)}), bf16[8,128,2048]{2,1,0:T(8,128)(2,1)}, u32[]{:S(2)}, u32[]{:S(2)}) %all-to-all-start.4) | async-done | bytes 4194336 | tf_op jit(solution)/shard_map/all_to_all | solution.py:133
  297.1 4.0 %fusion.22 = f32[128,2048]{1,0:T(8,128)} fusion(bf16[1024,2048]{1,0:T(8,128)(2,1)} %bitcast.23, s32[1024]{0:T(1024)S(1)} %bitcast.97, pred[1024]{0:T(1024)(128)(4,1)S(1)} %bitcast.102), kind=kOutput, calls=%fused_computation.41 | convolution fusion | flops 537133056 | bytes 5248000 | tf_op jit(solution)/shard_map/dot_general | solution.py:144
  301.1 0.0 reduce-scatter.8.cloned.1.call-update
  301.1 4.2 %fusion.4 = bf16[1,192,2048]{2,1,0:T(8,128)(2,1)} fusion(bf16[1024,192]{0,1:T(8,128)(2,1)S(1)} %get-tuple-element.10, bf16[1024,2048]{1,0:T(8,128)(2,1)} %bitcast.86), kind=kOutput, calls=%fused_computation.15 | convolution fusion | flops 805699584 | bytes 5373952 | tf_op jit(solution)/shard_map/dot_general | solution.py:16
  305.3 0.0 copy-done.2
  305.3 1.9 fusion.5
  307.2 0.0 copy-done.5
  307.2 4.3 %fusion.6 = bf16[1,192,2048]{2,1,0:T(8,128)(2,1)} fusion(bf16[1024,192]{0,1:T(8,128)(2,1)S(1)} %copy-done.5, bf16[1024,2048]{1,0:T(8,128)(2,1)} %bitcast.21, f32[1024]{0:T(1024)S(1)} %bitcast.109), kind=kOutput, calls=%fused_computation.17 | convolution fusion | flops 811991040 | bytes 5378048 | tf_op jit(solution)/shard_map/dot_general | solution.py:16
  311.6 1.4 copy.30
  313.0 1.6 convert_element_type.81
  314.6 14.8 %reduce-scatter.8.cloned.1.call-done = f32[128,512]{1,0:T(8,128)} async-done(((f32[128,2048]{1,0:T(8,128)}), f32[128,512]{1,0:T(8,128)}) %reduce-scatter.8.cloned.1.call-update) | async-done | bytes 262160 | tf_op jit(solution)/shard_map/reduce_scatter | solution.py:156
  329.4 1.6 convert_element_type.85
  (26 shorter events, 0.2 us)
Async XLA Ops:
  7.2 168.9 %copy-start = (bf16[1,192,2048]{2,1,0:T(8,128)(2,1)S(1)}, bf16[1,192,2048]{2,1,0:T(8,128)(2,1)}, u32[]{:S(2)}) copy-start(bf16[1,192,2048]{2,1,0:T(8,128)(2,1)} %param.12) | copy-start | bytes 2359300
  21.7 44.1 %all-to-all-start = ((bf16[8,1,128]{2,1,0:T(2,128)(2,1)}), bf16[8,1,128]{2,1,0:T(2,128)(2,1)S(1)}, u32[]{:S(2)}, u32[]{:S(2)}) async-start(bf16[8,1,128]{2,1,0:T(2,128)(2,1)} %copy.26), calls=%async_computation | async-start | bytes 8192 | tf_op jit(solution)/shard_map/all_to_all | solution.py:85
  122.3 4.7 %copy-start.4 = (bf16[1,192,2048]{2,1,0:T(8,128)(2,1)S(1)}, bf16[1,192,2048]{2,1,0:T(8,128)(2,1)}, u32[]{:S(2)}) copy-start(bf16[1,192,2048]{2,1,0:T(8,128)(2,1)} %param.11) | copy-start | bytes 2359300
  122.3 53.8 %all-to-all-start.3 = ((bf16[8,128,2048]{2,1,0:T(8,128)(2,1)}), bf16[8,128,2048]{2,1,0:T(8,128)(2,1)}, u32[]{:S(2)}, u32[]{:S(2)}) async-start(bf16[8,128,2048]{2,1,0:T(8,128)(2,1)} %bitcast.89), calls=%async_computation.4 | async-start | bytes 8388608 | tf_op jit(solution)/shard_map/all_to_all | solution.py:113
  127.0 4.8 %copy-start.1 = (bf16[8,128,2048]{2,1,0:T(8,128)(2,1)S(1)}, bf16[8,128,2048]{2,1,0:T(8,128)(2,1)}, u32[]{:S(2)}) copy-start(bf16[8,128,2048]{2,1,0:T(8,128)(2,1)} %all_to_all.36) | copy-start | bytes 12582916
  127.0 4.8 %copy-start.3 = (bf16[1,192,2048]{2,1,0:T(8,128)(2,1)S(1)}, bf16[1,192,2048]{2,1,0:T(8,128)(2,1)}, u32[]{:S(2)}) copy-start(bf16[1,192,2048]{2,1,0:T(8,128)(2,1)} %param.10) | copy-start | bytes 2359300
  181.9 7.8 %all-to-all-start.5 = ((bf16[8,1,128]{2,1,0:T(2,128)(2,1)}), bf16[8,1,128]{2,1,0:T(2,128)(2,1)S(1)}, u32[]{:S(2)}, u32[]{:S(2)}) async-start(bf16[8,1,128]{2,1,0:T(2,128)(2,1)} %copy.27), calls=%async_computation.7 | async-start | bytes 8192 | tf_op jit(solution)/shard_map/all_to_all | solution.py:140
  189.7 53.7 %all-to-all-start.2 = ((bf16[8,128,2048]{2,1,0:T(8,128)(2,1)}), bf16[8,128,2048]{2,1,0:T(8,128)(2,1)}, u32[]{:S(2)}, u32[]{:S(2)}) async-start(bf16[8,128,2048]{2,1,0:T(8,128)(2,1)} %bitcast.94), calls=%async_computation.2 | async-start | bytes 8388608 | tf_op jit(solution)/shard_map/all_to_all | solution.py:94
  243.4 53.7 %all-to-all-start.4 = ((bf16[8,128,2048]{2,1,0:T(8,128)(2,1)}), bf16[8,128,2048]{2,1,0:T(8,128)(2,1)}, u32[]{:S(2)}, u32[]{:S(2)}) async-start(bf16[8,128,2048]{2,1,0:T(8,128)(2,1)} %bitcast.91), calls=%async_computation.5 | async-start | bytes 8388608 | tf_op jit(solution)/shard_map/all_to_all | solution.py:133
  248.0 63.6 %reduce-scatter.10.cloned.1.call-start = ((), (), s32[]{:S(2)}) async-start(), calls=%async_computation.11 | async-start | bytes 81920
  253.5 59.4 %reduce-scatter.6.cloned.1.call-start = ((), (), s32[]{:S(2)}) async-start(), calls=%async_computation.9 | async-start | bytes 1310720 | tf_op jit(solution)/shard_map/reduce_scatter | solution.py:155
  257.5 71.9 %reduce-scatter.8.cloned.1.call-start = ((), (), s32[]{:S(2)}) async-start(), calls=%async_computation.10 | async-start | bytes 1310720 | tf_op jit(solution)/shard_map/reduce_scatter | solution.py:156
  301.1 4.2 %copy-start.2 = (bf16[8,128,2048]{2,1,0:T(8,128)(2,1)S(1)}, bf16[8,128,2048]{2,1,0:T(8,128)(2,1)}, u32[]{:S(2)}) copy-start(bf16[8,128,2048]{2,1,0:T(8,128)(2,1)} %all_to_all.36) | copy-start | bytes 12582916
  301.1 6.1 %copy-start.5 = (bf16[1024,192]{0,1:T(8,128)(2,1)S(1)}, bf16[1024,192]{0,1:T(8,128)(2,1)}, u32[]{:S(2)}) copy-start(bf16[1024,192]{0,1:T(8,128)(2,1)} %get-tuple-element.7) | copy-start | bytes 1179652
Sparse Core Ops, SparseCore 0:
  253.7 19.6 reduce-scatter.9
  275.8 25.3 reduce-scatter.5
  303.4 25.8 reduce-scatter.7
where the time goes:
time: 338 us
  waiting for transfers between devices  141 us (42%)
  blocking collectives  85.9 us (25%)
  matrix products  44.9 us (13%)
  local copies, waits for them, and re-layouts  23.2 us (7%)
  starting transfers between devices  22.6 us (7%)
  between operations  14 us (4%)
  other arithmetic  6.01 us (2%)
    all_to_all x1, blocking collectives, on_device(): lax.all_to_all(send_rows, 'dp', split_axis=0, concat_axis=0, tiled=True)  53.4 us
    all_to_all x1, waiting for transfers between devices, on_device(): lax.all_to_all(scaled.reshape(data_size, capacity, feature_width), 'dp',...  44.4 us
    all_to_all x1, waiting for transfers between devices, on_device(): lax.all_to_all(send_grads, 'dp', split_axis=0, concat_axis=0, tiled=True)  41.9 us
    all_to_all x1, waiting for transfers between devices, on_device(): lax.all_to_all(row_grad.reshape(data_size, capacity, feature_width), 'dp'...  39.6 us
    all_gather x1, blocking collectives, on_device(): lax.all_gather(tokens, 'expert', axis=1, tiled=True)  16.8 us
    all_gather x1, blocking collectives, on_device(): lax.all_gather(grad_output, 'expert', axis=1, tiled=True)  15.7 us
    reduce_scatter x1, waiting for transfers between devices, on_device(): lax.psum_scatter(token_sum, 'expert', scatter_dimension=1, tiled=True)  14.8 us
    dot_general x3, matrix products, contract_last(): lax.dot_general(left_side, right_side, (((1,), (1,)), ((), ())), preferre...  12.4 us
  transfers between devices with their start and end apart: 8, of which 5 were waited for; matrix products, arithmetic and copies ran while one was open for 15% of the time, Pallas kernels for 0%

commit v1 on v0

--- a/solution.py
+++ b/solution.py
@@ -33,7 +33,7 @@
     return (scaled, gate_act, up_act, hidden)
 
 
-def on_device(tokens, route_weight, expert_ids, gate_weight, up_weight, down_weight, grad_output):
+def slot_device(tokens, route_weight, expert_ids, gate_weight, up_weight, down_weight, grad_output):
     groups = lax.axis_size("expert")
     group_index = lax.axis_index("expert")
     data_size = lax.axis_size("dp")
@@ -166,6 +166,61 @@
     )
 
 
+def dense_device(tokens, route_weight, expert_ids, gate_weight, up_weight, down_weight, grad_output):
+    groups = lax.axis_size("expert")
+    group_index = lax.axis_index("expert")
+    data_size = lax.axis_size("dp")
+    exp_local = data_size // PIECES
+    experts = exp_local * groups
+    own_expert = group_index * exp_local + lax.axis_index("dp") // PIECES
+    gate_piece, up_piece, down_piece = gate_weight[0], up_weight[0], down_weight[0]
+    names = jnp.arange(experts, dtype=jnp.int32)
+    onehot = (expert_ids[:, :, None] == names).astype(jnp.float32)
+    dense_weight = jnp.sum(onehot * route_weight.astype(jnp.float32)[:, :, None], axis=1)
+    dense_weight = lax.all_gather(dense_weight, "dp", axis=0, tiled=True)
+    weight_col = lax.dynamic_slice_in_dim(dense_weight, own_expert, 1, axis=1)
+    gathered = lax.all_gather(tokens, "expert", axis=1, tiled=True)
+    full_tokens = lax.all_gather(gathered, "dp", axis=0, tiled=True)
+    gathered = lax.all_gather(grad_output, "expert", axis=1, tiled=True)
+    full_grad = lax.all_gather(gathered, "dp", axis=0, tiled=True)
+    gate_act = contract_last(full_tokens, gate_piece)
+    up_act = contract_last(full_tokens, up_piece)
+    active, slope = silu_parts(gate_act)
+    hidden = active * up_act
+    weighted = (weight_col * hidden).astype(jnp.bfloat16)
+    mixed = jnp.dot(weighted, down_piece, preferred_element_type=jnp.float32).astype(jnp.bfloat16)
+    into_hidden = contract_last(full_grad, down_piece)
+    route_terms = jnp.sum(into_hidden * hidden, axis=1, keepdims=True)
+    scaled = weight_col * into_hidden
+    gate_grad = (scaled * up_act * slope).astype(jnp.bfloat16)
+    up_grad = (scaled * active).astype(jnp.bfloat16)
+    row_grad = (
+        jnp.dot(gate_grad, gate_piece, preferred_element_type=jnp.float32)
+        + jnp.dot(up_grad, up_piece, preferred_element_type=jnp.float32)
+    ).astype(jnp.bfloat16)
+    grad_gate = contract_first(gate_grad, full_tokens).astype(jnp.bfloat16)[None]
+    grad_up = contract_first(up_grad, full_tokens).astype(jnp.bfloat16)[None]
+    grad_down = contract_first(weighted, full_grad).astype(jnp.bfloat16)[None]
+
+    def scatter(values, dim):
+        values = lax.psum_scatter(values, "dp", scatter_dimension=0, tiled=True)
+        return lax.psum_scatter(values, "expert", scatter_dimension=dim, tiled=True)
+
+    route_wide = jnp.where(names[None, :] == own_expert, route_terms, 0.0)
+    route_part = scatter(route_wide, 0)
+    rows = route_part.shape[0]
+    ids_part = lax.dynamic_slice_in_dim(expert_ids, group_index * rows, rows, axis=0)
+    onehot_part = (ids_part[:, :, None] == names).astype(jnp.float32)
+    grad_route = jnp.sum(onehot_part * route_part[:, None, :], axis=2)
+    return (scatter(mixed, 1), scatter(row_grad, 1), grad_route, grad_gate, grad_up, grad_down)
+
+
+def on_device(tokens, route_weight, expert_ids, *rest):
+    experts = lax.axis_size("dp") // PIECES * lax.axis_size("expert")
+    body = dense_device if experts == expert_ids.shape[1] else slot_device
+    return body(tokens, route_weight, expert_ids, *rest)
+
+
 def solution(mesh):
     return jax.shard_map(
         on_device,

time: 338 us -> 322 us (0.953)
  waiting for transfers between devices: 141 us -> 230 us
  blocking collectives: 85.9 us -> 45.3 us
  starting transfers between devices: 22.6 us -> 0.33 us
  local copies, waits for them, and re-layouts: 23.2 us -> 2.3 us
  matrix products: 44.9 us -> 26.5 us
    reduce_scatter x2 -> x5, waiting for transfers between devices: 14.8 us -> 175 us  [the longest x3 131 us: scatter(): values = lax.psum_scatter(values, 'dp', scatter_dimension=0, tiled=True)]
    all_to_all x5 -> x0, waiting for transfers between devices: 126 us -> none  [the longest x1 44.4 us: on_device(): lax.all_to_all(scaled.reshape(data_size, capacity, feature_width), 'dp',...]
    all_to_all x1 -> x0, blocking collectives: 53.4 us -> none  [on_device(): lax.all_to_all(send_rows, 'dp', split_axis=0, concat_axis=0, tiled=True)]
    all_gather x0 -> x2, waiting for transfers between devices: none -> 41.4 us  [the longest x1 32 us: dense_device(): full_grad = lax.all_gather(gathered, 'dp', axis=0, tiled=True)]
    all_to_all x5 -> x0, starting transfers between devices: 22.5 us -> none  [the longest x1 5.17 us: on_device(): lax.all_to_all(send_weight, 'dp', split_axis=0, concat_axis=0, tiled=True)]
    dot_general x6 -> x3, matrix products: 22.1 us -> 7.77 us  [the longest x1 3.25 us: dense_device(): jnp.dot(up_grad, up_piece, preferred_element_type=jnp.float32)]
    unnamed x4 -> x9, waiting for transfers between devices: 0.05 us -> 13.3 us
    all_gather x2 -> x3, blocking collectives: 32.4 us -> 45.3 us  [the longest x1 19.5 us: dense_device(): gathered = lax.all_gather(tokens, 'expert', axis=1, tiled=True)]
  transfers between devices with their start and end apart: 8 -> 8, of which waited for: 5 -> 8; matrix products, arithmetic and copies ran while one was open for 15% -> 8% of each run, Pallas kernels for 0% -> 0%
where the time goes in v1:
time: 322 us; the launch traced here: 321 us
  waiting for transfers between devices  230 us (71%)
  blocking collectives  45.3 us (14%)
  matrix products  26.5 us (8%)
  between operations  14.2 us (4%)
    reduce_scatter x3, waiting for transfers between devices, scatter(): values = lax.psum_scatter(values, 'dp', scatter_dimension=0, tiled=True)  131 us
    reduce_scatter x2, waiting for transfers between devices, scatter(): return lax.psum_scatter(values, 'expert', scatter_dimension=dim, tiled=True)  43.9 us
    all_gather x1, waiting for transfers between devices, dense_device(): full_grad = lax.all_gather(gathered, 'dp', axis=0, tiled=True)  32 us
    all_gather x1, blocking collectives, dense_device(): gathered = lax.all_gather(tokens, 'expert', axis=1, tiled=True)  19.5 us
    all_gather x1, blocking collectives, dense_device(): gathered = lax.all_gather(grad_output, 'expert', axis=1, tiled=True)  16.7 us
    unnamed x9, waiting for transfers between devices  13.3 us
    dot_general x3, matrix products, contract_last(): lax.dot_general(left_side, right_side, (((1,), (1,)), ((), ())), preferre...  10.8 us
    all_gather x1, waiting for transfers between devices, dense_device(): full_tokens = lax.all_gather(gathered, 'dp', axis=0, tiled=True)  9.36 us
  transfers between devices with their start and end apart: 8, of which 8 were waited for; matrix products, arithmetic and copies ran while one was open for 8% of the time, Pallas kernels for 0%

profile of v1, /device:TPU:0, one launch (start us, length us, event | category | flops | bytes accessed | tf_op | source)
XLA Modules:
  0.0 321.3 jit_solution(12690550985246331621)
XLA Ops:
  7.2 0.0 copy-start
  7.2 0.0 copy-start.3
  7.2 0.0 all-gather.3.cloned.1.call-start
  7.2 19.5 %all_gather.16 = bf16[128,2048]{1,0:T(8,128)(2,1)} all-gather(bf16[128,512]{1,0:T(8,128)(2,1)} %param.7), channel_id=1, replica_groups=mesh['dp'=8,'expert'=4] {'expert'}, dimensions={1}, use_global_device_ids=true | all-gather | bytes 655360 | tf_op jit(solution)/shard_map/all_gather | solution.py:182
  26.8 0.0 all-gather.3.cloned.1.call-update
  26.8 0.0 all-gather.5.cloned.1.call-start
  26.9 16.7 %all_gather.18 = bf16[128,2048]{1,0:T(8,128)(2,1)} all-gather(bf16[128,512]{1,0:T(8,128)(2,1)} %param.13), channel_id=1, replica_groups=mesh['dp'=8,'expert'=4] {'expert'}, dimensions={1}, use_global_device_ids=true | all-gather | bytes 655360 | tf_op jit(solution)/shard_map/all_gather | solution.py:184
  43.6 0.0 all-gather.5.cloned.1.call-update
  43.6 0.0 reduce-scatter.17.cloned.1.call-start
  43.7 0.7 convert_element_type.29
  44.3 0.7 select_reduce_fusion.1
  45.0 9.1 %all_gather.15 = f32[1024,8]{0,1:T(8,128)S(1)} all-gather(f32[128,8]{0,1:T(8,128)S(1)} %select_reduce_fusion.1), channel_id=1, replica_groups=mesh['dp'=8,'expert'=4] {'dp'}, dimensions={0}, use_global_device_ids=true | all-gather | bytes 36864 | tf_op jit(solution)/shard_map/all_gather | solution.py:180
  54.1 9.4 %all-gather.3.cloned.1.call-done = bf16[1024,2048]{1,0:T(8,128)(2,1)} async-done(((bf16[128,2048]{1,0:T(8,128)(2,1)}), bf16[1024,2048]{1,0:T(8,128)(2,1)}) %all-gather.3.cloned.1.call-update) | async-done | bytes 4194320 | tf_op jit(solution)/shard_map/all_gather | solution.py:183
  63.5 0.0 copy-start.1
  63.5 4.1 %fusion.7 = f32[1024,192]{0,1:T(8,128)S(1)} fusion(bf16[1024,2048]{1,0:T(8,128)(2,1)} %all-gather.3.cloned.1.call-done, bf16[1,192,2048]{2,1,0:T(8,128)(2,1)} %param.11), kind=kOutput, calls=%fused_computation.12 | convolution fusion | flops 805306368 | bytes 5767168 | tf_op jit(solution)/shard_map/dot_general | solution.py:10
  67.6 0.0 copy-done.3
  67.6 0.0 copy-done.1
  67.6 2.5 fusion.11
  70.1 32.0 %all-gather.5.cloned.1.call-done = bf16[1024,2048]{1,0:T(8,128)(2,1)} async-done(((bf16[128,2048]{1,0:T(8,128)(2,1)}), bf16[1024,2048]{1,0:T(8,128)(2,1)}) %all-gather.5.cloned.1.call-update) | async-done | bytes 4194320 | tf_op jit(solution)/shard_map/all_gather | solution.py:185
  102.1 0.0 copy-done
  102.1 4.2 %multiply_reduce_fusion = (f32[1024]{0:T(1024)S(1)}, bf16[1024,192]{0,1:T(8,128)(2,1)S(1)}, bf16[1024,192]{0,1:T(8,128)(2,1)S(1)}, bf16[1024,192]{0,1:T(8,128)(2,1)S(1)}) fusion(f32[1024,192]{0,1:T(8,128)S(1)} %fusion.7, f32[1024,192]{0,1:T(8,128)} %fusion.11, f32[1024]{0:T(1024)S(1)} %bitcast.37, bf16[1024,2048]{1,0:T(8,128)(2,1)} %all-gather.5.cloned.1.call-done, ...), kind=kOutput, calls=%fused_computation.18 | convolution fusion | flops 809040896 | bytes 7741440 | tf_op jit(solution)/shard_map/dot_general | solution.py:10
  106.3 0.7 broadcast_select_fusion
  107.0 0.0 reduce-scatter.17.cloned.1.call-update
  107.0 0.0 reduce-scatter.9.cloned.1.call-start
  107.1 3.2 %convolution_convert_fusion = bf16[1024,2048]{1,0:T(8,128)(2,1)} fusion(bf16[1024,192]{0,1:T(8,128)(2,1)S(1)} %get-tuple-element.8, bf16[1,192,2048]{2,1,0:T(8,128)(2,1)S(1)} %copy-done), kind=kOutput, calls=%fused_computation.1 | convolution fusion | flops 807403520 | bytes 5373952 | tf_op jit(solution)/shard_map/dot_general | solution.py:191
  110.3 0.0 reduce-scatter.9.cloned.1.call-update
  110.4 0.0 reduce-scatter.13.cloned.1.call-start
  110.4 0.0 copy-start.4
  110.4 1.3 fusion.9
  111.7 0.0 copy-done.4
  111.7 3.2 %add_convert_fusion = bf16[1024,2048]{1,0:T(8,128)(2,1)} fusion(f32[1024,2048]{1,0:T(8,128)S(1)} %fusion.9, bf16[1024,192]{0,1:T(8,128)(2,1)S(1)} %get-tuple-element.9, bf16[1,192,2048]{2,1,0:T(8,128)(2,1)S(1)} %copy-done.4), kind=kOutput, calls=%fused_computation | convolution fusion | flops 809500672 | bytes 13762560 | tf_op jit(solution)/shard_map/dot_general | solution.py:199
  115.0 0.0 copy-start.5
  115.0 0.0 reduce-scatter.13.cloned.1.call-update
  115.0 0.0 reduce-scatter.19.cloned.1.call-start
  115.0 23.5 %reduce-scatter.17.cloned.1.call-done = f32[128,8]{0,1:T(8,128)} async-done(((f32[1024,8]{0,1:T(8,128)}), f32[128,8]{0,1:T(8,128)}) %reduce-scatter.17.cloned.1.call-update) | async-done | bytes 4112 | tf_op jit(solution)/shard_map/reduce_scatter | solution.py:206
  138.5 1.4 copy.19
  139.9 0.0 reduce-scatter.19.cloned.1.call-update
  139.9 0.0 reduce-scatter.11.cloned.1.call-start
  140.0 53.5 %reduce-scatter.9.cloned.1.call-done = bf16[128,2048]{1,0:T(8,128)(2,1)} async-done(((bf16[1024,2048]{1,0:T(8,128)(2,1)}), bf16[128,2048]{1,0:T(8,128)(2,1)}) %reduce-scatter.9.cloned.1.call-update) | async-done | bytes 524304 | tf_op jit(solution)/shard_map/reduce_scatter | solution.py:206
  193.4 0.0 reduce-scatter.11.cloned.1.call-update
  193.5 0.0 reduce-scatter.15.cloned.1.call-start
  193.5 0.0 copy-done.5
  193.5 0.1 constant_dynamic-slice_fusion
  193.6 54.4 %reduce-scatter.13.cloned.1.call-done = bf16[128,2048]{1,0:T(8,128)(2,1)} async-done(((bf16[1024,2048]{1,0:T(8,128)(2,1)}), bf16[128,2048]{1,0:T(8,128)(2,1)}) %reduce-scatter.13.cloned.1.call-update) | async-done | bytes 524304 | tf_op jit(solution)/shard_map/reduce_scatter | solution.py:206
  248.0 0.0 reduce-scatter.15.cloned.1.call-update
  248.0 0.0 copy-start.2
  248.0 4.2 %fusion.2 = bf16[1,192,2048]{2,1,0:T(8,128)(2,1)} fusion(bf16[1024,192]{0,1:T(8,128)(2,1)S(1)} %get-tuple-element.8, bf16[1024,2048]{1,0:T(8,128)(2,1)} %all-gather.5.cloned.1.call-done), kind=kOutput, calls=%fused_computation.7 | convolution fusion | flops 805699584 | bytes 5373952 | tf_op jit(solution)/shard_map/dot_general | solution.py:16
  252.2 0.0 copy-done.2
  252.2 1.9 fusion
  254.1 1.9 fusion.1
  256.0 13.2 %reduce-scatter.19.cloned.1.call-done = f32[32,8]{1,0:T(8,128)} async-done(((f32[128,8]{1,0:T(8,128)}), f32[32,8]{1,0:T(8,128)}) %reduce-scatter.19.cloned.1.call-update) | async-done | bytes 1040
  269.2 0.8 copy.20
  270.0 0.6 select_reduce_fusion
  270.6 21.3 %reduce-scatter.11.cloned.1.call-done = bf16[128,512]{1,0:T(8,128)(2,1)} async-done(((bf16[128,2048]{1,0:T(8,128)(2,1)}), bf16[128,512]{1,0:T(8,128)(2,1)}) %reduce-scatter.11.cloned.1.call-update) | async-done | bytes 131088 | tf_op jit(solution)/shard_map/reduce_scatter | solution.py:207
  291.9 22.6 %reduce-scatter.15.cloned.1.call-done = bf16[128,512]{1,0:T(8,128)(2,1)} async-done(((bf16[128,2048]{1,0:T(8,128)(2,1)}), bf16[128,512]{1,0:T(8,128)(2,1)}) %reduce-scatter.15.cloned.1.call-update) | async-done | bytes 131088 | tf_op jit(solution)/shard_map/reduce_scatter | solution.py:207
  (2 shorter events, 0.0 us)
Async XLA Ops:
  7.2 94.9 %copy-start = (bf16[1,192,2048]{2,1,0:T(8,128)(2,1)S(1)}, bf16[1,192,2048]{2,1,0:T(8,128)(2,1)}, u32[]{:S(2)}) copy-start(bf16[1,192,2048]{2,1,0:T(8,128)(2,1)} %param.12) | copy-start | bytes 2359300
  7.2 60.4 %copy-start.3 = (bf16[1,192,2048]{2,1,0:T(8,128)(2,1)S(1)}, bf16[1,192,2048]{2,1,0:T(8,128)(2,1)}, u32[]{:S(2)}) copy-start(bf16[1,192,2048]{2,1,0:T(8,128)(2,1)} %param.10) | copy-start | bytes 2359300
  7.2 56.3 %all-gather.3.cloned.1.call-start = ((), (), s32[]{:S(2)}) async-start(), calls=%async_computation.6 | async-start | bytes 4718592 | tf_op jit(solution)/shard_map/all_gather | solution.py:183
  26.8 75.3 %all-gather.5.cloned.1.call-start = ((), (), s32[]{:S(2)}) async-start(), calls=%async_computation.9 | async-start | bytes 4718592 | tf_op jit(solution)/shard_map/all_gather | solution.py:185
  43.6 94.9 %reduce-scatter.17.cloned.1.call-start = ((), (), s32[]{:S(2)}) async-start(), calls=%async_computation.12 | async-start | bytes 36864 | tf_op jit(solution)/shard_map/reduce_scatter | solution.py:206
  63.5 4.1 %copy-start.1 = (bf16[1024,2048]{1,0:T(8,128)(2,1)S(1)}, bf16[1024,2048]{1,0:T(8,128)(2,1)}, u32[]{:S(2)}) copy-start(bf16[1024,2048]{1,0:T(8,128)(2,1)} %all-gather.3.cloned.1.call-done) | copy-start | bytes 12582916
  107.0 86.4 %reduce-scatter.9.cloned.1.call-start = ((), (), s32[]{:S(2)}) async-start(), calls=%async_computation.7 | async-start | bytes 4718592 | tf_op jit(solution)/shard_map/reduce_scatter | solution.py:206
  110.4 137.6 %reduce-scatter.13.cloned.1.call-start = ((), (), s32[]{:S(2)}) async-start(), calls=%async_computation.10 | async-start | bytes 4718592 | tf_op jit(solution)/shard_map/reduce_scatter | solution.py:206
  110.4 1.3 copy-start.4
  115.0 78.6 %copy-start.5 = (s32[128,8]{0,1:T(8,128)S(1)}, s32[128,8]{0,1:T(8,128)}, u32[]{:S(2)}) copy-start(s32[128,8]{0,1:T(8,128)} %param.9) | copy-start | bytes 12292
  115.0 154.2 %reduce-scatter.19.cloned.1.call-start = ((), (), s32[]{:S(2)}) async-start(), calls=%async_computation.13 | async-start | bytes 81920
  139.9 151.9 %reduce-scatter.11.cloned.1.call-start = ((), (), s32[]{:S(2)}) async-start(), calls=%async_computation.8 | async-start | bytes 655360 | tf_op jit(solution)/shard_map/reduce_scatter | solution.py:207
  193.5 121.0 %reduce-scatter.15.cloned.1.call-start = ((), (), s32[]{:S(2)}) async-start(), calls=%async_computation.11 | async-start | bytes 655360 | tf_op jit(solution)/shard_map/reduce_scatter | solution.py:207
  248.0 4.2 %copy-start.2 = (bf16[1024,2048]{1,0:T(8,128)(2,1)S(1)}, bf16[1024,2048]{1,0:T(8,128)(2,1)}, u32[]{:S(2)}) copy-start(bf16[1024,2048]{1,0:T(8,128)(2,1)} %all-gather.3.cloned.1.call-done) | copy-start | bytes 12582916
Sparse Core Ops, SparseCore 0:
  26.9 36.5 all-gather.2
  65.4 36.6 all-gather.4
  107.2 31.2 reduce-scatter.16
  142.1 51.3 reduce-scatter.8
  196.6 51.3 reduce-scatter.12
  250.2 18.9 reduce-scatter.18
  272.0 19.7 reduce-scatter.10
  294.7 19.7 reduce-scatter.14

commit v2 on v0

--- a/solution.py
+++ b/solution.py
@@ -1,6 +1,8 @@
 import jax
 import jax.numpy as jnp
 from jax import lax
+from jax.experimental import pallas as pl
+from jax.experimental.pallas import tpu as pltpu
 from jax.sharding import PartitionSpec as P
 
 PIECES = 4
@@ -33,7 +35,7 @@
     return (scaled, gate_act, up_act, hidden)
 
 
-def on_device(tokens, route_weight, expert_ids, gate_weight, up_weight, down_weight, grad_output):
+def slot_device(tokens, route_weight, expert_ids, gate_weight, up_weight, down_weight, grad_output):
     groups = lax.axis_size("expert")
     group_index = lax.axis_index("expert")
     data_size = lax.axis_size("dp")
@@ -166,6 +168,395 @@
     )
 
 
+MESH = pl.DeviceIdType.MESH
+GATHER_ORDER = (0, 1, 3, 2)
+SCATTER_ORDER = (2, 1, 3, 0)
+
+
+def remote(src, dst, sems, index, device):
+    return pltpu.make_async_remote_copy(
+        src_ref=src,
+        dst_ref=dst,
+        send_sem=sems.at[(0,) + index],
+        recv_sem=sems.at[(1,) + index],
+        device_id=device,
+        device_id_type=MESH,
+    )
+
+
+def dense_kernel(
+    tok_ref, rw_ref, ids_ref, wg_ref, wu_ref, wd_ref, gy_ref,
+    mixed_ref, token_ref, route_ref, gg_ref, gu_ref, gd_ref,
+    acts, parts, weights, wide, gate, up, into, hw, gg, ug, turned,
+    half_in, full_in, z_out, z_in, z_own, route, route_in, route_sum, route_z, wg_out, wg_in,
+    s_z, s_plane, s_fwd, s_wide, s_wt, s_local, s_r1, s_r2, s_r3, s_rt, s_rz, s_wg,
+):
+    f32, bf16 = jnp.float32, jnp.bfloat16
+    rows, feat = tok_ref.shape
+    unit = wg_ref.shape[1]
+    topk = ids_ref.shape[1]
+    half = rows // 2
+    quarters = acts.shape[1]
+    d, z = lax.axis_index("dp"), lax.axis_index("expert")
+    core, x, y = lax.rem(d, 2), lax.rem(d // 2, 2), d // 4
+    x_dev = (y * 4 + (1 - x) * 2 + core, z)
+    y_dev = ((1 - y) * 4 + x * 2 + core, z)
+    diag_dev = ((1 - y) * 4 + (1 - x) * 2 + core, z)
+    twin = (y * 4 + x * 2 + (1 - core), z)
+    expert = z * (lax.axis_size("dp") // PIECES) + d // PIECES
+
+    def quarter(r):
+        return lax.rem(z + r, quarters)
+
+    def z_dev(r):
+        return (d, quarter(r))
+
+    barrier = pltpu.get_barrier_semaphore()
+    others = [x_dev, y_dev, diag_dev, twin] + [z_dev(r) for r in range(1, quarters)]
+    for dev in others:
+        pl.semaphore_signal(barrier, inc=1, device_id=dev, device_id_type=MESH)
+    pl.semaphore_wait(barrier, len(others))
+
+    own, at_x, at_y, at_d = (pl.ds(i * rows, rows) for i in range(4))
+    d_top, d_low = pl.ds(3 * rows, half), pl.ds(3 * rows + half, half)
+    x_top, x_low = pl.ds(rows, half), pl.ds(rows + half, half)
+    y_top, y_low = pl.ds(2 * rows, half), pl.ds(2 * rows + half, half)
+    started = []
+
+    def go(copy):
+        copy.start()
+        started.append(copy)
+
+    def z_send(a, s):
+        block = acts.at[a, z, own]
+        return remote(block, block, s_z, (a, quarters - 1 - s), z_dev(s))
+
+    def z_arrive(a, r):
+        block = acts.at[a, quarter(r), own]
+        remote(block, block, s_z, (a, r - 1), z_dev(r)).wait_recv()
+
+    def plane(a, r):
+        q = quarter(r)
+        src = acts.at[a, q, own]
+        return (
+            remote(src, acts.at[a, q, at_x], s_plane, (a, 0, r), x_dev),
+            remote(src, acts.at[a, q, at_y], s_plane, (a, 1, r), y_dev),
+        )
+
+    def forward(a, r):
+        q = quarter(r)
+        return (
+            remote(acts.at[a, q, x_top], acts.at[a, q, d_top], s_fwd, (a, 0, r), y_dev),
+            remote(acts.at[a, q, y_low], acts.at[a, q, d_low], s_fwd, (a, 1, r), x_dev),
+        )
+
+    def send_plane(a, r):
+        for copy in plane(a, r):
+            go(copy)
+
+    def pass_on(a, r):
+        for arrived, onward in zip(plane(a, r), forward(a, r)):
+            arrived.wait_recv()
+            go(onward)
+
+    def complete(a, r):
+        for copy in forward(a, r):
+            copy.wait_recv()
+
+    acts[0, z, own, :] = tok_ref[...]
+    acts[1, z, own, :] = gy_ref[...]
+    for s in (1, 3, 2):
+        go(z_send(0, s))
+    send_plane(0, 0)
+    local, lent = [], []
+    for m, ref in enumerate((wg_ref, wu_ref, wd_ref)):
+        copy = pltpu.make_async_copy(ref.at[0], weights.at[m, pl.ds(0, unit)], s_local.at[m])
+        copy.start()
+        local.append(copy)
+        lent.append(remote(ref.at[0], weights.at[m, pl.ds(unit, unit)], s_wt, (m,), twin))
+        go(lent[m])
+
+    lane = lax.broadcasted_iota(jnp.int32, (rows, 128), 1)
+    ids, rw = ids_ref[...], rw_ref[...].astype(f32)
+    spread = jnp.zeros((rows, 128), f32)
+    for k in range(topk):
+        spread = spread + jnp.where(lane == ids[:, k : k + 1], rw[:, k : k + 1], 0.0)
+    wide[own, :] = spread
+    wide_copies = [
+        remote(wide.at[own], wide.at[place], s_wide, (i,), dev)
+        for i, (place, dev) in enumerate(((at_x, x_dev), (at_y, y_dev), (at_d, diag_dev)))
+    ]
+    for copy in wide_copies:
+        go(copy)
+    for s in (1, 3, 2):
+        go(z_send(1, s))
+    for r in GATHER_ORDER[1:]:
+        z_arrive(0, r)
+        send_plane(0, r)
+    for m in range(3):
+        local[m].wait()
+        lent[m].wait_recv()
+
+    def columns(q):
+        return pl.ds(pl.multiple_of(q * feat, feat), feat)
+
+    def add_forward(i, r):
+        q = quarter(r)
+        for total, m in ((gate, 0), (up, 1)):
+            term = contract_last(acts[0, q], weights[m, :, columns(q)])
+            total[...] = term if i == 0 else total[...] + term
+
+    for i, r in enumerate(GATHER_ORDER):
+        pass_on(0, r)
+        if i > 0:
+            z_arrive(1, r)
+        send_plane(1, r)
+        if i > 0:
+            complete(0, GATHER_ORDER[i - 1])
+            add_forward(i - 1, GATHER_ORDER[i - 1])
+    complete(0, GATHER_ORDER[-1])
+    add_forward(len(GATHER_ORDER) - 1, GATHER_ORDER[-1])
+    for copy in wide_copies:
+        copy.wait_recv()
+
+    def block_rows(b):
+        return pl.ds(pl.multiple_of(b * rows, rows), rows)
+
+    def scale_of(b):
+        return jnp.sum(jnp.where(lane == expert, wide[block_rows(b), :], 0.0), axis=1, keepdims=True)
+
+    @pl.loop(0, 4)
+    def _(b):
+        at = block_rows(b)
+        active, _slope = silu_parts(gate[at, :])
+        weighted = scale_of(b) * (active * up[at, :])
+        hw[at, :] = weighted.astype(bf16)
+        turned[2, :, at] = weighted.T.astype(bf16)
+
+    def first(a, r):
+        q = quarter(r)
+        return (
+            remote(parts.at[a, q, d_top], half_in.at[a, 0, r], s_r1, (a, 0, r), x_dev),
+            remote(parts.at[a, q, d_low], half_in.at[a, 1, r], s_r1, (a, 1, r), y_dev),
+        )
+
+    def second(a, r):
+        q = quarter(r)
+        return (
+            remote(parts.at[a, q, at_x], full_in.at[a, 0, r], s_r2, (a, 0, r), x_dev),
+            remote(parts.at[a, q, at_y], full_in.at[a, 1, r], s_r2, (a, 1, r), y_dev),
+        )
+
+    def send_first(a, r):
+        for copy in first(a, r):
+            go(copy)
+
+    def add_first(a, r):
+        q = quarter(r)
+        for i, (copy, place) in enumerate(zip(first(a, r), (y_top, x_low))):
+            copy.wait_recv()
+            here = parts[a, q, place, :].astype(f32) + half_in[a, i, r].astype(f32)
+            parts[a, q, place, :] = here.astype(bf16)
+        for copy in second(a, r):
+            go(copy)
+
+    def third(a, r):
+        return remote(z_out.at[a, r - 1], z_in.at[a, quarters - 1 - r], s_r3, (a, quarters - 1 - r), z_dev(r))
+
+    def add_second(a, r):
+        for copy in second(a, r):
+            copy.wait_recv()
+        total = parts[a, quarter(r), own, :].astype(f32)
+        total = total + full_in[a, 0, r].astype(f32) + full_in[a, 1, r].astype(f32)
+        if r == 0:
+            z_own[a] = total
+        else:
+            z_out[a, r - 1] = total.astype(bf16)
+            go(third(a, r))
+
+    def finish(a, out_ref):
+        total = z_own[a]
+        for r in range(1, quarters):
+            slot = z_in.at[a, r - 1]
+            remote(slot, slot, s_r3, (a, r - 1), z_dev(r)).wait_recv()
+            total = total + z_in[a, r - 1].astype(f32)
+        out_ref[...] = total.astype(bf16)
+
+    for near, r in zip(GATHER_ORDER, SCATTER_ORDER):
+        q = quarter(r)
+        pass_on(1, near)
+        parts[0, q] = jnp.dot(
+            hw[...], weights[2, :, columns(q)], preferred_element_type=f32
+        ).astype(bf16)
+        send_first(0, r)
+
+    for i, (near, r) in enumerate(zip(GATHER_ORDER, SCATTER_ORDER)):
+        q = quarter(near)
+        complete(1, near)
+        term = contract_last(acts[1, q], weights[2, :, columns(q)])
+        into[...] = term if i == 0 else into[...] + term
+        add_first(0, r)
+
+    @pl.loop(0, 4)
+    def _(b):
+        at = block_rows(b)
+        gate_act, up_act, back = gate[at, :], up[at, :], into[at, :]
+        active, slope = silu_parts(gate_act)
+        term = jnp.sum(back * (active * up_act), axis=1, keepdims=True)
+        route[at, :] = jnp.where(lane == expert, term, 0.0)
+        scaled = scale_of(b) * back
+        gate_grad, up_grad = scaled * up_act * slope, scaled * active
+        gg[at, :] = gate_grad.astype(bf16)
+        ug[at, :] = up_grad.astype(bf16)
+        turned[0, :, at] = gate_grad.T.astype(bf16)
+        turned[1, :, at] = up_grad.T.astype(bf16)
+
+    for r in SCATTER_ORDER:
+        q = quarter(r)
+        total = jnp.dot(gg[...], weights[0, :, columns(q)], preferred_element_type=f32)
+        total = total + jnp.dot(ug[...], weights[1, :, columns(q)], preferred_element_type=f32)
+        parts[1, q] = total.astype(bf16)
+        send_first(1, r)
+        add_second(0, r)
+
+    route_copies = [
+        remote(route.at[place], route_in.at[i], s_rt, (i,), dev)
+        for i, (place, dev) in enumerate(((at_x, x_dev), (at_y, y_dev), (at_d, diag_dev)))
+    ]
+    for copy in route_copies:
+        go(copy)
+
+    lent_grads = []
+    for m in range(3):
+        @pl.loop(0, quarters)
+        def _(q, m=m):
+            wg_out[m, :, columns(q)] = jnp.dot(
+                turned[m, pl.ds(unit, unit), :], acts[m // 2, q], preferred_element_type=f32
+            ).astype(bf16)
+
+        lent_grads.append(remote(wg_out.at[m], wg_in.at[m], s_wg, (m,), twin))
+        go(lent_grads[m])
+
+    for r in SCATTER_ORDER:
+        add_first(1, r)
+
+    for copy in route_copies:
+        copy.wait_recv()
+    route_sum[...] = route[own, :] + route_in[0] + route_in[1] + route_in[2]
+    slab = rows // quarters
+
+    def slab_of(q):
+        return pl.ds(pl.multiple_of(q * slab, slab), slab)
+
+    for s in range(1, quarters):
+        go(remote(route_sum.at[slab_of(quarter(s))], route_z.at[quarters - 1 - s], s_rz, (quarters - 1 - s,), z_dev(s)))
+
+    for m, out_ref in enumerate((gg_ref, gu_ref, gd_ref)):
+        lent_grads[m].wait_recv()
+
+        @pl.loop(0, quarters)
+        def _(q, m=m, out_ref=out_ref):
+            total = jnp.dot(turned[m, pl.ds(0, unit), :], acts[m // 2, q], preferred_element_type=f32)
+            out_ref[0, :, columns(q)] = (total + wg_in[m, :, columns(q)].astype(f32)).astype(bf16)
+
+    finish(0, mixed_ref)
+    for r in SCATTER_ORDER:
+        add_second(1, r)
+
+    total = route_sum[slab_of(z), :]
+    for r in range(1, quarters):
+        slot = route_z.at[r - 1]
+        remote(slot, slot, s_rz, (r - 1,), z_dev(r)).wait_recv()
+        total = total + route_z[r - 1]
+    names = ids_ref[slab_of(z), :]
+    lane_slab = lax.broadcasted_iota(jnp.int32, (slab, 128), 1)
+    lane_k = lax.broadcasted_iota(jnp.int32, (slab, topk), 1)
+    picked = jnp.zeros((slab, topk), f32)
+    for k in range(topk):
+        value = jnp.sum(jnp.where(lane_slab == names[:, k : k + 1], total, 0.0), axis=1, keepdims=True)
+        picked = jnp.where(lane_k == k, value, picked)
+    route_ref[...] = picked
+    finish(1, token_ref)
+    for copy in started:
+        copy.wait_send()
+
+
+def dense_device(tokens, route_weight, expert_ids, gate_weight, up_weight, down_weight, grad_output):
+    quarters = lax.axis_size("expert")
+    rows, feat = tokens.shape
+    unit, width = gate_weight.shape[1:]
+    topk = expert_ids.shape[1]
+    f32, bf16 = jnp.float32, jnp.bfloat16
+    vmem = pl.BlockSpec(memory_space=pltpu.VMEM)
+    hbm = pl.BlockSpec(memory_space=pl.ANY)
+    every, both, half = 4 * rows, 2 * unit, rows // 2
+    dma = pltpu.SemaphoreType.DMA
+    grads = jax.ShapeDtypeStruct((1, unit, width), bf16)
+    return pl.pallas_call(
+        dense_kernel,
+        out_shape=(
+            jax.ShapeDtypeStruct((rows, feat), bf16),
+            jax.ShapeDtypeStruct((rows, feat), bf16),
+            jax.ShapeDtypeStruct((rows // quarters, topk), f32),
+            grads,
+            grads,
+            grads,
+        ),
+        in_specs=[vmem, vmem, vmem, hbm, hbm, hbm, vmem],
+        out_specs=(vmem,) * 6,
+        scratch_shapes=[
+            pltpu.VMEM((2, quarters, every, feat), bf16),
+            pltpu.VMEM((2, quarters, every, feat), bf16),
+            pltpu.VMEM((3, both, width), bf16),
+            pltpu.VMEM((every, 128), f32),
+            pltpu.VMEM((every, both), f32),
+            pltpu.VMEM((every, both), f32),
+            pltpu.VMEM((every, both), f32),
+            pltpu.VMEM((every, both), bf16),
+            pltpu.VMEM((every, both), bf16),
+            pltpu.VMEM((every, both), bf16),
+            pltpu.VMEM((3, both, every), bf16),
+            pltpu.VMEM((2, 2, quarters, half, feat), bf16),
+            pltpu.VMEM((2, 2, quarters, rows, feat), bf16),
+            pltpu.VMEM((2, quarters - 1, rows, feat), bf16),
+            pltpu.VMEM((2, quarters - 1, rows, feat), bf16),
+            pltpu.VMEM((2, rows, feat), f32),
+            pltpu.VMEM((every, 128), f32),
+            pltpu.VMEM((3, rows, 128), f32),
+            pltpu.VMEM((rows, 128), f32),
+            pltpu.VMEM((quarters - 1, rows // quarters, 128), f32),
+            pltpu.VMEM((3, unit, width), bf16),
+            pltpu.VMEM((3, unit, width), bf16),
+            dma((2, 2, quarters - 1)),
+            dma((2, 2, 2, quarters)),
+            dma((2, 2, 2, quarters)),
+            dma((2, 3)),
+            dma((2, 3)),
+            dma((3,)),
+            dma((2, 2, 2, quarters)),
+            dma((2, 2, 2, quarters)),
+            dma((2, 2, quarters - 1)),
+            dma((2, 3)),
+            dma((2, quarters - 1)),
+            dma((2, 3)),
+        ],
+        compiler_params=pltpu.CompilerParams(
+            collective_id=0, has_side_effects=True, vmem_limit_bytes=52 * 2**20
+        ),
+        cost_estimate=pl.CostEstimate(
+            flops=18 * every * both * width, bytes_accessed=12 * unit * width, transcendentals=2 * every * both
+        ),
+    )(tokens, route_weight, expert_ids, gate_weight, up_weight, down_weight, grad_output)
+
+
+def on_device(tokens, route_weight, expert_ids, *rest):
+    shape = (lax.axis_size("dp"), lax.axis_size("expert"))
+    experts = shape[0] // PIECES * shape[1]
+    dense = shape == (8, 4) and experts == expert_ids.shape[1]
+    body = dense_device if dense else slot_device
+    return body(tokens, route_weight, expert_ids, *rest)
+
+
 def solution(mesh):
     return jax.shard_map(
         on_device,

time: 338 us -> 101 us (0.30)
  waiting for transfers between devices: 141 us -> 0 us
  Pallas kernels: 0 us -> 91.4 us
  blocking collectives: 85.9 us -> 0 us
  matrix products: 44.9 us -> 0 us
  starting transfers between devices: 22.6 us -> 0 us
  local copies, waits for them, and re-layouts: 23.2 us -> 8.4 us
  between operations: 14 us -> 0.66 us
  other arithmetic: 6.01 us -> 0 us
    all_to_all x5 -> x0, waiting for transfers between devices: 126 us -> none  [the longest x1 44.4 us: on_device(): lax.all_to_all(scaled.reshape(data_size, capacity, feature_width), 'dp',...]
    pallas_call x0 -> x1, Pallas kernels: none -> 91.4 us  [dense_device(): pl.pallas_call(dense_kernel, out_shape=(jax.ShapeDtypeStruct((rows, feat)...]
    all_to_all x1 -> x0, blocking collectives: 53.4 us -> none  [on_device(): lax.all_to_all(send_rows, 'dp', split_axis=0, concat_axis=0, tiled=True)]
    dot_general x12 -> x0, matrix products: 44.9 us -> none  [the longest x3 12.4 us: contract_last(): lax.dot_general(left_side, right_side, (((1,), (1,)), ((), ())), preferre...]
    all_gather x2 -> x0, blocking collectives: 32.4 us -> none  [the longest x1 16.8 us: on_device(): lax.all_gather(tokens, 'expert', axis=1, tiled=True)]
    all_to_all x5 -> x0, starting transfers between devices: 22.5 us -> none  [the longest x1 5.17 us: on_device(): lax.all_to_all(send_weight, 'dp', split_axis=0, concat_axis=0, tiled=True)]
    reduce_scatter x2 -> x0, waiting for transfers between devices: 14.8 us -> none  [the longest x1 14.8 us: on_device(): lax.psum_scatter(token_sum, 'expert', scatter_dimension=1, tiled=True)]
    scatter x2 -> x0, local copies, waits for them, and re-layouts: 8.61 us -> none  [the longest x1 4.3 us: on_device(): jnp.zeros((slot_count,), jnp.int32).at[slot_pos].set(row_index, mode='drop')]
  transfers between devices with their start and end apart: 8 -> 0, of which waited for: 5 -> 0; matrix products, arithmetic and copies ran while one was open for 15% -> 0% of each run, Pallas kernels for 0% -> 0%
where the time goes in v2:
time: 101 us; the launch traced here: 100 us
  Pallas kernels  91.4 us (90%)
  local copies, waits for them, and re-layouts  8.4 us (8%)
    pallas_call x1, Pallas kernels, dense_device(): pl.pallas_call(dense_kernel, out_shape=(jax.ShapeDtypeStruct((rows, feat)...  91.4 us
    unnamed x17, local copies, waits for them, and re-layouts  7.73 us

profile of v2, /device:TPU:0, one launch (start us, length us, event | category | flops | bytes accessed | tf_op | source)
XLA Modules:
  0.0 100.4 jit_solution(17955695216484067068)
XLA Ops:
  0.6 0.0 copy-start.4
  0.6 0.8 copy.13.rw_ref
  1.4 0.0 copy-done.4
  1.4 0.1 copy.14.ids_ref
  1.6 0.0 copy-start
  1.6 0.9 copy-done
  2.5 0.0 copy-start.1
  2.5 0.9 copy-done.1
  3.4 91.4 %shard_map.118 = (bf16[128,512]{1,0:T(8,128)(2,1)S(1)}, bf16[128,512]{1,0:T(8,128)(2,1)S(1)}, f32[32,8]{1,0:T(8,128)S(1)}, bf16[1,192,2048]{2,1,0:T(8,128)(2,1)S...) custom-call(bf16[128,512]{1,0:T(8,128)(2,1)S(1)} %copy-done, bf16[128,8]{1,0:T(8,128)(2,1)S(1)} %copy.13.rw_ref, ...), custom_call_target="tpu_custom_call" | custom-call | flops 7247757312 | bytes 4718592 | tf_op jit(solution)/shard_map/pallas_call | solution.py:495
  94.7 0.7 copy.15
  95.4 0.7 copy.21
  96.0 0.7 copy.22
  96.7 0.0 copy-start.3
  96.7 0.9 copy.23
  97.6 0.5 copy-done.3
  98.1 0.0 copy-start.2
  98.1 0.9 copy.24
  99.0 0.5 copy-done.2
  99.5 0.9 copy.25
Async XLA Ops:
  0.6 0.8 copy-start.4
  1.6 0.9 copy-start
  2.5 0.9 copy-start.1
  96.7 1.4 %copy-start.3 = (bf16[1,192,2048]{2,1,0:T(8,128)(2,1)S(1)}, bf16[1,192,2048]{2,1,0:T(8,128)(2,1)}, u32[]{:S(2)}) copy-start(bf16[1,192,2048]{2,1,0:T(8,128)(2,1)} %get-tuple-element.22) | copy-start | bytes 2359300
  98.1 1.4 %copy-start.2 = (bf16[1,192,2048]{2,1,0:T(8,128)(2,1)S(1)}, bf16[1,192,2048]{2,1,0:T(8,128)(2,1)}, u32[]{:S(2)}) copy-start(bf16[1,192,2048]{2,1,0:T(8,128)(2,1)} %get-tuple-element.23) | copy-start | bytes 2359300

commit v3 on v2

--- a/solution.py
+++ b/solution.py
@@ -187,14 +187,14 @@
 def dense_kernel(
     tok_ref, rw_ref, ids_ref, wg_ref, wu_ref, wd_ref, gy_ref,
     mixed_ref, token_ref, route_ref, gg_ref, gu_ref, gd_ref,
-    acts, parts, weights, wide, gate, up, into, hw, gg, ug, turned,
+    acts, parts, weights, wide, names_wide, gate, up, into, hw, gg, ug, turned,
     half_in, full_in, z_out, z_in, z_own, route, route_in, route_sum, route_z, wg_out, wg_in,
     s_z, s_plane, s_fwd, s_wide, s_wt, s_local, s_r1, s_r2, s_r3, s_rt, s_rz, s_wg,
 ):
     f32, bf16 = jnp.float32, jnp.bfloat16
     rows, feat = tok_ref.shape
     unit = wg_ref.shape[1]
-    topk = ids_ref.shape[1]
+    topk = ids_ref.shape[0]
     half = rows // 2
     quarters = acts.shape[1]
     d, z = lax.axis_index("dp"), lax.axis_index("expert")
@@ -228,8 +228,7 @@
         started.append(copy)
 
     def z_send(a, s):
-        block = acts.at[a, z, own]
-        return remote(block, block, s_z, (a, quarters - 1 - s), z_dev(s))
+        return remote((tok_ref, gy_ref)[a], acts.at[a, z, own], s_z, (a, quarters - 1 - s), z_dev(s))
 
     def z_arrive(a, r):
         block = acts.at[a, quarter(r), own]
@@ -237,7 +236,7 @@
 
     def plane(a, r):
         q = quarter(r)
-        src = acts.at[a, q, own]
+        src = (tok_ref, gy_ref)[a] if r == 0 else acts.at[a, q, own]
         return (
             remote(src, acts.at[a, q, at_x], s_plane, (a, 0, r), x_dev),
             remote(src, acts.at[a, q, at_y], s_plane, (a, 1, r), y_dev),
@@ -263,12 +262,14 @@
         for copy in forward(a, r):
             copy.wait_recv()
 
-    acts[0, z, own, :] = tok_ref[...]
-    acts[1, z, own, :] = gy_ref[...]
     for s in (1, 3, 2):
         go(z_send(0, s))
     send_plane(0, 0)
+    send_plane(1, 0)
     local, lent = [], []
+    for a, ref in enumerate((tok_ref, gy_ref)):
+        local.append(pltpu.make_async_copy(ref, acts.at[a, z, own], s_local.at[3 + a]))
+        local[a].start()
     for m, ref in enumerate((wg_ref, wu_ref, wd_ref)):
         copy = pltpu.make_async_copy(ref.at[0], weights.at[m, pl.ds(0, unit)], s_local.at[m])
         copy.start()
@@ -278,24 +279,30 @@
 
     lane = lax.broadcasted_iota(jnp.int32, (rows, 128), 1)
     ids, rw = ids_ref[...], rw_ref[...].astype(f32)
-    spread = jnp.zeros((rows, 128), f32)
+    level = lax.broadcasted_iota(jnp.int32, (128, rows), 0)
+    spread, named = jnp.zeros((128, rows), f32), jnp.zeros((128, rows), f32)
     for k in range(topk):
-        spread = spread + jnp.where(lane == ids[:, k : k + 1], rw[:, k : k + 1], 0.0)
-    wide[own, :] = spread
+        spread = spread + jnp.where(level == ids[k : k + 1, :], rw[k : k + 1, :], 0.0)
+        named = named + jnp.where(level == k, ids[k : k + 1, :].astype(f32), 0.0)
+    wide[own, :] = spread.T
+    names_wide[...] = named.T
     wide_copies = [
         remote(wide.at[own], wide.at[place], s_wide, (i,), dev)
         for i, (place, dev) in enumerate(((at_x, x_dev), (at_y, y_dev), (at_d, diag_dev)))
     ]
     for copy in wide_copies:
         go(copy)
+    for i, r in enumerate(GATHER_ORDER[1:]):
+        z_arrive(0, r)
+        send_plane(0, r)
+        if i < 2:
+            pass_on(i, 0)
     for s in (1, 3, 2):
         go(z_send(1, s))
-    for r in GATHER_ORDER[1:]:
-        z_arrive(0, r)
-        send_plane(0, r)
-    for m in range(3):
-        local[m].wait()
-        lent[m].wait_recv()
+    for copy in local:
+        copy.wait()
+    for copy in lent:
+        copy.wait_recv()
 
     def columns(q):
         return pl.ds(pl.multiple_of(q * feat, feat), feat)
@@ -307,11 +314,10 @@
             total[...] = term if i == 0 else total[...] + term
 
     for i, r in enumerate(GATHER_ORDER):
-        pass_on(0, r)
         if i > 0:
+            pass_on(0, r)
             z_arrive(1, r)
-        send_plane(1, r)
-        if i > 0:
+            send_plane(1, r)
             complete(0, GATHER_ORDER[i - 1])
             add_forward(i - 1, GATHER_ORDER[i - 1])
     complete(0, GATHER_ORDER[-1])
@@ -384,7 +390,8 @@
 
     for near, r in zip(GATHER_ORDER, SCATTER_ORDER):
         q = quarter(r)
-        pass_on(1, near)
+        if near > 0:
+            pass_on(1, near)
         parts[0, q] = jnp.dot(
             hw[...], weights[2, :, columns(q)], preferred_element_type=f32
         ).astype(bf16)
@@ -417,6 +424,7 @@
         total = total + jnp.dot(ug[...], weights[1, :, columns(q)], preferred_element_type=f32)
         parts[1, q] = total.astype(bf16)
         send_first(1, r)
+    for r in SCATTER_ORDER:
         add_second(0, r)
 
     route_copies = [
@@ -448,8 +456,10 @@
     def slab_of(q):
         return pl.ds(pl.multiple_of(q * slab, slab), slab)
 
+    slab_copies = []
     for s in range(1, quarters):
-        go(remote(route_sum.at[slab_of(quarter(s))], route_z.at[quarters - 1 - s], s_rz, (quarters - 1 - s,), z_dev(s)))
+        slab_copies.append(remote(route_sum.at[slab_of(quarter(s))], route_z.at[quarters - 1 - s], s_rz, (quarters - 1 - s,), z_dev(s)))
+        slab_copies[-1].start()
 
     for m, out_ref in enumerate((gg_ref, gu_ref, gd_ref)):
         lent_grads[m].wait_recv()
@@ -468,17 +478,30 @@
         slot = route_z.at[r - 1]
         remote(slot, slot, s_rz, (r - 1,), z_dev(r)).wait_recv()
         total = total + route_z[r - 1]
-    names = ids_ref[slab_of(z), :]
+    for copy in slab_copies:
+        copy.wait_send()
+    names = names_wide[slab_of(z), :]
     lane_slab = lax.broadcasted_iota(jnp.int32, (slab, 128), 1)
-    lane_k = lax.broadcasted_iota(jnp.int32, (slab, topk), 1)
-    picked = jnp.zeros((slab, topk), f32)
+    picked = jnp.zeros((slab, 128), f32)
     for k in range(topk):
-        value = jnp.sum(jnp.where(lane_slab == names[:, k : k + 1], total, 0.0), axis=1, keepdims=True)
-        picked = jnp.where(lane_k == k, value, picked)
-    route_ref[...] = picked
+        match = lane_slab.astype(f32) == names[:, k : k + 1]
+        value = jnp.sum(jnp.where(match, total, 0.0), axis=1, keepdims=True)
+        picked = jnp.where(lane_slab == k, value, picked)
+    route_sum[pl.ds(0, slab), :] = picked
+    route_ref[...] = route_sum[...].T[:topk, :slab]
     finish(1, token_ref)
     for copy in started:
         copy.wait_send()
+
+
+def deliver(*refs):
+    sems = refs[-1]
+    count = len(refs) // 2
+    copies = [pltpu.make_async_copy(refs[i], refs[count + i], sems.at[i]) for i in range(count)]
+    for copy in copies:
+        copy.start()
+    for copy in copies:
+        copy.wait()
 
 
 def dense_device(tokens, route_weight, expert_ids, gate_weight, up_weight, down_weight, grad_output):
@@ -489,26 +512,28 @@
     f32, bf16 = jnp.float32, jnp.bfloat16
     vmem = pl.BlockSpec(memory_space=pltpu.VMEM)
     hbm = pl.BlockSpec(memory_space=pl.ANY)
+    stay = pl.BlockSpec(memory_space=pltpu.HBM)
     every, both, half = 4 * rows, 2 * unit, rows // 2
     dma = pltpu.SemaphoreType.DMA
     grads = jax.ShapeDtypeStruct((1, unit, width), bf16)
-    return pl.pallas_call(
+    results = pl.pallas_call(
         dense_kernel,
         out_shape=(
             jax.ShapeDtypeStruct((rows, feat), bf16),
             jax.ShapeDtypeStruct((rows, feat), bf16),
-            jax.ShapeDtypeStruct((rows // quarters, topk), f32),
+            jax.ShapeDtypeStruct((topk, rows // quarters), f32),
             grads,
             grads,
             grads,
         ),
-        in_specs=[vmem, vmem, vmem, hbm, hbm, hbm, vmem],
+        in_specs=[stay, vmem, vmem, stay, stay, stay, stay],
         out_specs=(vmem,) * 6,
         scratch_shapes=[
             pltpu.VMEM((2, quarters, every, feat), bf16),
             pltpu.VMEM((2, quarters, every, feat), bf16),
             pltpu.VMEM((3, both, width), bf16),
             pltpu.VMEM((every, 128), f32),
+            pltpu.VMEM((rows, 128), f32),
             pltpu.VMEM((every, both), f32),
             pltpu.VMEM((every, both), f32),
             pltpu.VMEM((every, both), f32),
@@ -532,7 +557,7 @@
             dma((2, 2, 2, quarters)),
             dma((2, 3)),
             dma((2, 3)),
-            dma((3,)),
+            dma((5,)),
             dma((2, 2, 2, quarters)),
             dma((2, 2, 2, quarters)),
             dma((2, 2, quarters - 1)),
@@ -541,12 +566,21 @@
             dma((2, 3)),
         ],
         compiler_params=pltpu.CompilerParams(
-            collective_id=0, has_side_effects=True, vmem_limit_bytes=52 * 2**20
+            collective_id=0, has_side_effects=True, vmem_limit_bytes=51 * 2**20
         ),
         cost_estimate=pl.CostEstimate(
             flops=18 * every * both * width, bytes_accessed=12 * unit * width, transcendentals=2 * every * both
         ),
-    )(tokens, route_weight, expert_ids, gate_weight, up_weight, down_weight, grad_output)
+    )(tokens, route_weight.T, expert_ids.T, gate_weight, up_weight, down_weight, grad_output)
+    count = len(results)
+    mixed, token_part, route_part, *weight_grads = pl.pallas_call(
+        deliver,
+        out_shape=tuple(jax.ShapeDtypeStruct(v.shape, v.dtype) for v in results),
+        in_specs=[hbm] * count,
+        out_specs=(hbm,) * count,
+        scratch_shapes=[dma((count,))],
+    )(*results)
+    return (mixed, token_part, route_part.T, *weight_grads)
 
 
 def on_device(tokens, route_weight, expert_ids, *rest):

time: 101 us -> 175 us (1.73)
  Pallas kernels: 91.4 us -> 167 us
    pallas_call x0 -> x1, Pallas kernels: none -> 80.7 us  [dense_device(): pl.pallas_call(deliver, out_shape=tuple((jax.ShapeDtypeStruct(v.shape, v....]
    pallas_call x1, Pallas kernels: 91.4 us -> 86 us  [dense_device(): pl.pallas_call(dense_kernel, out_shape=(jax.ShapeDtypeStruct((rows, feat)...]
    unnamed x17 -> x20, local copies, waits for them, and re-layouts: 7.73 us -> 7.69 us
where the time goes in v3:
time: 175 us
  Pallas kernels  167 us (95%)
  local copies, waits for them, and re-layouts  7.69 us (4%)
    pallas_call x1, Pallas kernels, dense_device(): pl.pallas_call(dense_kernel, out_shape=(jax.ShapeDtypeStruct((rows, feat)...  86 us
    pallas_call x1, Pallas kernels, dense_device(): pl.pallas_call(deliver, out_shape=tuple((jax.ShapeDtypeStruct(v.shape, v....  80.7 us
    unnamed x20, local copies, waits for them, and re-layouts  7.69 us

profile of v3, /device:TPU:0, one launch (start us, length us, event | category | flops | bytes accessed | tf_op | source)
XLA Modules:
  0.0 175.1 jit_solution(3443493665020671803)
XLA Ops:
  0.6 0.0 copy-start.9
  0.6 0.7 copy-done.9
  1.3 0.0 copy-start.6
  1.3 0.9 copy-done.6
  2.2 0.0 copy-start.7
  2.2 0.9 copy-done.7
  3.1 0.0 copy-start.8
  3.1 0.7 copy-done.8
  3.8 86.0 %shard_map.118 = (bf16[128,512]{1,0:T(8,128)(2,1)S(1)}, bf16[128,512]{1,0:T(8,128)(2,1)S(1)}, f32[8,32]{1,0:T(8,128)S(1)}, bf16[1,192,2048]{2,1,0:T(8,128)(2,1)S...) custom-call(bf16[128,512]{1,0:T(8,128)(2,1)S(1)} %copy-done.6, bf16[8,128]{1,0:T(8,128)(2,1)S(1)} %bitcast.4, ...), custom_call_target="tpu_custom_call" | custom-call | flops 7247757312 | bytes 4718592 | tf_op jit(solution)/shard_map/pallas_call | solution.py:519
  89.8 0.0 copy-start
  89.9 0.9 copy-done
  90.7 0.0 copy-start.1
  90.7 0.9 copy-done.1
  91.7 0.0 copy-start.2
  91.7 0.9 copy-done.2
  92.5 0.0 copy-start.3
  92.5 0.6 copy-done.3
  93.2 0.0 copy-start.4
  93.2 0.6 copy-done.4
  93.8 0.0 copy-start.5
  93.8 0.6 copy-done.5
  94.4 80.7 %shard_map.119 = (bf16[128,512]{1,0:T(8,128)(2,1)}, bf16[128,512]{1,0:T(8,128)(2,1)}, f32[8,32]{1,0:T(8,128)}, bf16[1,192,2048]{2,1,0:T(8,128)(2,1)}, bf16[1,192...) custom-call(bf16[128,512]{1,0:T(8,128)(2,1)} %copy-done.3, bf16[128,512]{1,0:T(8,128)(2,1)} %copy-done.4, ...), custom_call_target="tpu_custom_call" | custom-call | tf_op jit(solution)/shard_map/pallas_call | solution.py:576
Async XLA Ops:
  0.6 0.7 copy-start.9
  1.3 0.9 copy-start.6
  2.2 0.9 copy-start.7
  3.1 0.7 copy-start.8
  89.8 0.9 copy-start
  90.7 0.9 copy-start.1
  91.7 0.9 copy-start.2
  92.5 0.6 copy-start.3
  93.2 0.6 copy-start.4
  93.8 0.6 copy-start.5

commit v4 on v3

--- a/solution.py
+++ b/solution.py
@@ -424,9 +424,6 @@
         total = total + jnp.dot(ug[...], weights[1, :, columns(q)], preferred_element_type=f32)
         parts[1, q] = total.astype(bf16)
         send_first(1, r)
-    for r in SCATTER_ORDER:
-        add_second(0, r)
-
     route_copies = [
         remote(route.at[place], route_in.at[i], s_rt, (i,), dev)
         for i, (place, dev) in enumerate(((at_x, x_dev), (at_y, y_dev), (at_d, diag_dev)))
@@ -446,6 +443,8 @@
         go(lent_grads[m])
 
     for r in SCATTER_ORDER:
+        add_second(0, r)
+    for r in SCATTER_ORDER:
         add_first(1, r)
 
     for copy in route_copies:
@@ -469,10 +468,10 @@
             total = jnp.dot(turned[m, pl.ds(0, unit), :], acts[m // 2, q], preferred_element_type=f32)
             out_ref[0, :, columns(q)] = (total + wg_in[m, :, columns(q)].astype(f32)).astype(bf16)
 
+        add_second(1, SCATTER_ORDER[m])
+
+    add_second(1, SCATTER_ORDER[3])
     finish(0, mixed_ref)
-    for r in SCATTER_ORDER:
-        add_second(1, r)
-
     total = route_sum[slab_of(z), :]
     for r in range(1, quarters):
         slot = route_z.at[r - 1]
@@ -495,13 +494,9 @@
 
 
 def deliver(*refs):
-    sems = refs[-1]
     count = len(refs) // 2
-    copies = [pltpu.make_async_copy(refs[i], refs[count + i], sems.at[i]) for i in range(count)]
-    for copy in copies:
-        copy.start()
-    for copy in copies:
-        copy.wait()
+    for src, dst in zip(refs[:count], refs[count:]):
+        dst[...] = src[...]
 
 
 def dense_device(tokens, route_weight, expert_ids, gate_weight, up_weight, down_weight, grad_output):
@@ -512,7 +507,6 @@
     f32, bf16 = jnp.float32, jnp.bfloat16
     vmem = pl.BlockSpec(memory_space=pltpu.VMEM)
     hbm = pl.BlockSpec(memory_space=pl.ANY)
-    stay = pl.BlockSpec(memory_space=pltpu.HBM)
     every, both, half = 4 * rows, 2 * unit, rows // 2
     dma = pltpu.SemaphoreType.DMA
     grads = jax.ShapeDtypeStruct((1, unit, width), bf16)
@@ -526,7 +520,7 @@
             grads,
             grads,
         ),
-        in_specs=[stay, vmem, vmem, stay, stay, stay, stay],
+        in_specs=[hbm, vmem, vmem, hbm, hbm, hbm, hbm],
         out_specs=(vmem,) * 6,
         scratch_shapes=[
             pltpu.VMEM((2, quarters, every, feat), bf16),
@@ -566,7 +560,7 @@
             dma((2, 3)),
         ],
         compiler_params=pltpu.CompilerParams(
-            collective_id=0, has_side_effects=True, vmem_limit_bytes=51 * 2**20
+            collective_id=0, has_side_effects=True, vmem_limit_bytes=60 * 2**20
         ),
         cost_estimate=pl.CostEstimate(
             flops=18 * every * both * width, bytes_accessed=12 * unit * width, transcendentals=2 * every * both
@@ -576,9 +570,9 @@
     mixed, token_part, route_part, *weight_grads = pl.pallas_call(
         deliver,
         out_shape=tuple(jax.ShapeDtypeStruct(v.shape, v.dtype) for v in results),
-        in_specs=[hbm] * count,
-        out_specs=(hbm,) * count,
-        scratch_shapes=[dma((count,))],
+        in_specs=[vmem] * count,
+        out_specs=(vmem,) * count,
+        compiler_params=pltpu.CompilerParams(vmem_limit_bytes=60 * 2**20),
     )(*results)
     return (mixed, token_part, route_part.T, *weight_grads)
 

time: 175 us -> 91.8 us (0.52)
  Pallas kernels: 167 us -> 91 us
  local copies, waits for them, and re-layouts: 7.69 us -> 0 us
    pallas_call x1, Pallas kernels: 80.7 us -> 3.24 us  [dense_device(): pl.pallas_call(deliver, out_shape=tuple((jax.ShapeDtypeStruct(v.shape, v....]
    unnamed x20 -> x0, local copies, waits for them, and re-layouts: 7.69 us -> none
where the time goes in v4:
time: 91.8 us; the launch traced here: 91.7 us
  Pallas kernels  91 us (99%)
    pallas_call x1, Pallas kernels, dense_device(): pl.pallas_call(dense_kernel, out_shape=(jax.ShapeDtypeStruct((rows, feat)...  87.8 us
    pallas_call x1, Pallas kernels, dense_device(): pl.pallas_call(deliver, out_shape=tuple((jax.ShapeDtypeStruct(v.shape, v....  3.24 us

profile of v4, /device:TPU:0, one launch (start us, length us, event | category | flops | bytes accessed | tf_op | source)
XLA Modules:
  0.0 91.7 jit_solution(5317264365352227200)
XLA Ops:
  0.6 87.8 %shard_map.118 = (bf16[128,512]{1,0:T(8,128)(2,1)}, bf16[128,512]{1,0:T(8,128)(2,1)}, f32[8,32]{1,0:T(8,128)}, bf16[1,192,2048]{2,1,0:T(8,128)(2,1)}, bf16[1,192...) custom-call(bf16[128,512]{1,0:T(8,128)(2,1)} %tok_ref.1, bf16[8,128]{1,0:T(8,128)(2,1)} %bitcast.5, s32[8,128]{1,0:T(8,128)} %bitcast.3, ...), custom_call_target="tpu_custom_call" | custom-call | flops 7247757312 | bytes 4718592 | tf_op jit(solution)/shard_map/pallas_call | solution.py:513
  88.4 3.2 %shard_map.119 = (bf16[128,512]{1,0:T(8,128)(2,1)}, bf16[128,512]{1,0:T(8,128)(2,1)}, f32[8,32]{1,0:T(8,128)}, bf16[1,192,2048]{2,1,0:T(8,128)(2,1)}, bf16[1,192...) custom-call(bf16[128,512]{1,0:T(8,128)(2,1)} %get-tuple-element.18.refs_0_, ...), custom_call_target="tpu_custom_call" | custom-call | tf_op jit(solution)/shard_map/pallas_call | solution.py:570

commit v5 on v4

--- a/solution.py
+++ b/solution.py
@@ -444,7 +444,7 @@
 
     for r in SCATTER_ORDER:
         add_second(0, r)
-    for r in SCATTER_ORDER:
+    for r in SCATTER_ORDER[:2]:
         add_first(1, r)
 
     for copy in route_copies:
@@ -468,6 +468,8 @@
             total = jnp.dot(turned[m, pl.ds(0, unit), :], acts[m // 2, q], preferred_element_type=f32)
             out_ref[0, :, columns(q)] = (total + wg_in[m, :, columns(q)].astype(f32)).astype(bf16)
 
+        if m < 2:
+            add_first(1, SCATTER_ORDER[m + 2])
         add_second(1, SCATTER_ORDER[m])
 
     add_second(1, SCATTER_ORDER[3])

time: 91.8 us -> 91.8 us (level)
  no operation moved by 1% of the time
where the time goes in v5:
time: 91.8 us; the launch traced here: 91.7 us
  Pallas kernels  91 us (99%)
    pallas_call x1, Pallas kernels, dense_device(): pl.pallas_call(dense_kernel, out_shape=(jax.ShapeDtypeStruct((rows, feat)...  87.8 us
    pallas_call x1, Pallas kernels, dense_device(): pl.pallas_call(deliver, out_shape=tuple((jax.ShapeDtypeStruct(v.shape, v....  3.24 us

profile of v5, /device:TPU:0, one launch (start us, length us, event | category | flops | bytes accessed | tf_op | source)
XLA Modules:
  0.0 91.7 jit_solution(394010772330223257)
XLA Ops:
  0.6 87.8 %shard_map.118 = (bf16[128,512]{1,0:T(8,128)(2,1)}, bf16[128,512]{1,0:T(8,128)(2,1)}, f32[8,32]{1,0:T(8,128)}, bf16[1,192,2048]{2,1,0:T(8,128)(2,1)}, bf16[1,192...) custom-call(bf16[128,512]{1,0:T(8,128)(2,1)} %tok_ref.1, bf16[8,128]{1,0:T(8,128)(2,1)} %bitcast.5, s32[8,128]{1,0:T(8,128)} %bitcast.3, ...), custom_call_target="tpu_custom_call" | custom-call | flops 7247757312 | bytes 4718592 | tf_op jit(solution)/shard_map/pallas_call | solution.py:515
  88.4 3.2 %shard_map.119 = (bf16[128,512]{1,0:T(8,128)(2,1)}, bf16[128,512]{1,0:T(8,128)(2,1)}, f32[8,32]{1,0:T(8,128)}, bf16[1,192,2048]{2,1,0:T(8,128)(2,1)}, bf16[1,192...) custom-call(bf16[128,512]{1,0:T(8,128)(2,1)} %get-tuple-element.18.refs_0_, ...), custom_call_target="tpu_custom_call" | custom-call | tf_op jit(solution)/shard_map/pallas_call | solution.py:572

commit v6 on v5

--- a/solution.py
+++ b/solution.py
@@ -297,8 +297,9 @@
         send_plane(0, r)
         if i < 2:
             pass_on(i, 0)
-    for s in (1, 3, 2):
-        go(z_send(1, s))
+        if i == 1:
+            for s in (1, 3, 2):
+                go(z_send(1, s))
     for copy in local:
         copy.wait()
     for copy in lent:
@@ -316,10 +317,11 @@
     for i, r in enumerate(GATHER_ORDER):
         if i > 0:
             pass_on(0, r)
-            z_arrive(1, r)
-            send_plane(1, r)
             complete(0, GATHER_ORDER[i - 1])
             add_forward(i - 1, GATHER_ORDER[i - 1])
+    for r in GATHER_ORDER[1:]:
+        z_arrive(1, r)
+        send_plane(1, r)
     complete(0, GATHER_ORDER[-1])
     add_forward(len(GATHER_ORDER) - 1, GATHER_ORDER[-1])
     for copy in wide_copies:

time: 91.8 us -> 92.9 us (1.012)
  Pallas kernels: 91 us -> 92.1 us
    pallas_call x1, Pallas kernels: 87.8 us -> 88.8 us  [dense_device(): pl.pallas_call(dense_kernel, out_shape=(jax.ShapeDtypeStruct((rows, feat)...]
where the time goes in v6:
time: 92.9 us; the launch traced here: 92.7 us
  Pallas kernels  92.1 us (99%)
    pallas_call x1, Pallas kernels, dense_device(): pl.pallas_call(dense_kernel, out_shape=(jax.ShapeDtypeStruct((rows, feat)...  88.8 us
    pallas_call x1, Pallas kernels, dense_device(): pl.pallas_call(deliver, out_shape=tuple((jax.ShapeDtypeStruct(v.shape, v....  3.24 us

profile of v6, /device:TPU:0, one launch (start us, length us, event | category | flops | bytes accessed | tf_op | source)
XLA Modules:
  0.0 92.7 jit_solution(13334653368586260737)
XLA Ops:
  0.6 88.8 %shard_map.118 = (bf16[128,512]{1,0:T(8,128)(2,1)}, bf16[128,512]{1,0:T(8,128)(2,1)}, f32[8,32]{1,0:T(8,128)}, bf16[1,192,2048]{2,1,0:T(8,128)(2,1)}, bf16[1,192...) custom-call(bf16[128,512]{1,0:T(8,128)(2,1)} %tok_ref.1, bf16[8,128]{1,0:T(8,128)(2,1)} %bitcast.5, s32[8,128]{1,0:T(8,128)} %bitcast.3, ...), custom_call_target="tpu_custom_call" | custom-call | flops 7247757312 | bytes 4718592 | tf_op jit(solution)/shard_map/pallas_call | solution.py:517
  89.5 3.2 %shard_map.119 = (bf16[128,512]{1,0:T(8,128)(2,1)}, bf16[128,512]{1,0:T(8,128)(2,1)}, f32[8,32]{1,0:T(8,128)}, bf16[1,192,2048]{2,1,0:T(8,128)(2,1)}, bf16[1,192...) custom-call(bf16[128,512]{1,0:T(8,128)(2,1)} %get-tuple-element.18.refs_0_, ...), custom_call_target="tpu_custom_call" | custom-call | tf_op jit(solution)/shard_map/pallas_call | solution.py:574
